TPU v7x, 128 devices: a whole 4x4x4 slice. The times are simulated.
128 devices in a mesh: gx: 16 (over y, x), gy: 8 (over z, core).
Axes of the slice: x: 4, y: 4, z: 4, core: 2. Of those that a mesh axis runs over, the one named last changes fastest.
Arguments:
- features: bfloat16 [64, 64, 64, 128], P('gx', 'gy'), may hold values from -6 to 6
- cell_count: int32 [64, 64], P('gx', 'gy'), may hold values from 32 to 128
- near_mask: int32 [64, 64, 9], P('gx', 'gy'), may hold values 0 or 1
- near_tiles: bfloat16 [64, 64, 9, 128, 128], P('gx', 'gy'), may hold values from -0.1875 to 0.1875
- projection_basis: bfloat16 [64, 64, 32, 128], P('gx', 'gy'), may hold values from -0.5 to 0.5
- expand_basis: bfloat16 [64, 64, 32, 128], P('gx', 'gy'), may hold values from -1 to 1
- far_source: int32 [16, 8, 128], P('gx', 'gy'), may hold values from 0 to 31
- far_owner: int32 [16, 8, 128, 1], P('gx', 'gy'), may hold values from 0 to 127; in each aligned block of 128 rows (0 to 127, 128 to 255, ..., all dimensions but the last counted through in order) at most 2 rows name the same one
- far_cell: int32 [16, 8, 128], P('gx', 'gy'), may hold values from 0 to 31
- distant_pair_matrix: bfloat16 [16, 8, 128, 1024], P('gx', 'gy'), may hold values from -1 to 1
- mixing: bfloat16 [2, 64, 64], replicated, may hold values from -0.75 to 0.75
Outputs:
- result: bfloat16 [64, 64, 64, 128], P('gx', 'gy')
Inputs may be any that keep to these rules, and one draw needn't show every extreme that they name: `far_owner`: among the far pairs of one device no owner is named more than 2 times, and one owner is named exactly 2 times on some devices.
All inputs are finite; a program needn't handle non-finite values. No bound on the sum of `near_mask` on one device may be relied on, other than what follows from the above.
Results may differ from a plain program's by a relative error of at most 0.0076.
Values may be sent and summed in bfloat16 or wider, within the bound.
A program may use at most 64 MiB of HBM per device.

v0:
```python
import jax
import jax.numpy as jnp
from jax import lax
from jax.sharding import PartitionSpec as P

LAYERS = 2


def extended(cells, sides, width):
    for axis, dim in sides:
        count = lax.axis_size(axis)
        head = lax.slice_in_dim(cells, 0, width, axis=dim)
        tail = lax.slice_in_dim(cells, cells.shape[dim] - width, cells.shape[dim], axis=dim)
        cells = jnp.concatenate(
            [
                lax.ppermute(tail, axis, [(i, (i + 1) % count) for i in range(count)]),
                cells,
                lax.ppermute(head, axis, [((i + 1) % count, i) for i in range(count)]),
            ],
            axis=dim,
        )
    return cells


def shards(
    features,
    cell_count,
    near_mask,
    near_tiles,
    projection_basis,
    expand_basis,
    far_source,
    far_owner,
    far_cell,
    distant_pair_matrix,
    mixing,
):
    cells_x, cells_y, chans, slots = features.shape
    rank = projection_basis.shape[2]
    cells = cells_x * cells_y
    pairs = far_source.shape[2]
    wide_x = lax.axis_size("gx")
    wide_y = lax.axis_size("gy")
    device_list = wide_x * wide_y
    capacity = max(2, 2 * pairs // device_list)
    live = (jnp.arange(slots, dtype=jnp.int32)[None, None, :] < cell_count[:, :, None]).astype(
        jnp.float32
    )
    x = (features.astype(jnp.float32) * live[:, :, None, :]).astype(jnp.bfloat16)
    owner = far_owner[0, 0, :, 0]
    source = far_source[0, 0]
    target_cell = far_cell[0, 0]
    pair_linkage = distant_pair_matrix[0, 0].reshape(pairs, rank, rank)
    onehot = (owner[:, None] == jnp.arange(device_list, dtype=jnp.int32)[None, :]).astype(jnp.int32)
    previous_state = jnp.cumsum(onehot, axis=0) - onehot
    position = owner * capacity + jnp.sum(previous_state * onehot, axis=1)
    weights_mask = near_mask.astype(jnp.float32)
    for layer in range(LAYERS):
        padded = extended(x, (("gx", 0), ("gy", 1)), 1)
        near = jnp.zeros((cells_x, cells_y, chans, slots), jnp.float32)
        for dx in (-1, 0, 1):
            for dy in (-1, 0, 1):
                offset = 3 * (dx + 1) + dy + 1
                shifted = padded[1 + dx : 1 + dx + cells_x, 1 + dy : 1 + dy + cells_y]
                part = jnp.einsum(
                    "abcj,abji->abci",
                    shifted,
                    near_tiles[:, :, offset],
                    preferred_element_type=jnp.float32,
                )
                near = near + weights_mask[:, :, offset][:, :, None, None] * part
        coef = jnp.einsum(
            "abcp,abrp->abcr", x, projection_basis, preferred_element_type=jnp.float32
        ).astype(jnp.bfloat16)
        picked_entries = coef.reshape(cells, chans, rank)[source]
        term = jnp.einsum(
            "nik,nku->niu", picked_entries, pair_linkage, preferred_element_type=jnp.float32
        ).astype(jnp.bfloat16)
        outbox = (
            jnp.zeros((device_list * capacity, chans * rank), jnp.bfloat16)
            .at[position]
            .set(term.reshape(pairs, chans * rank))
        )
        labels = jnp.zeros((device_list * capacity,), jnp.int32).at[position].set(target_cell)
        inbox, incoming_labels = (
            lax.all_to_all(outbox, ("gx", "gy"), split_axis=0, concat_axis=0, tiled=True),
            lax.all_to_all(labels, ("gx", "gy"), split_axis=0, concat_axis=0, tiled=True),
        )
        selection_mask = (
            incoming_labels[:, None] == jnp.arange(cells, dtype=jnp.int32)[None, :]
        ).astype(jnp.bfloat16)
        summed = jnp.einsum("sk,sf->kf", selection_mask, inbox, preferred_element_type=jnp.float32)
        gathered = summed.astype(jnp.bfloat16).reshape(cells_x, cells_y, chans, rank)
        far = jnp.einsum(
            "abcr,abrp->abcp", gathered, expand_basis, preferred_element_type=jnp.float32
        )
        mixed = jnp.einsum("dc,abcp->abdp", mixing[layer], x, preferred_element_type=jnp.float32)
        hidden = mixed + near + far
        x = (jax.nn.gelu(hidden, approximate=False) * live[:, :, None, :]).astype(jnp.bfloat16)
    return x


def solution(mesh):
    placed = (
        P("gx", "gy", None, None),
        P("gx", "gy"),
        P("gx", "gy", None),
        P("gx", "gy", None, None, None),
        P("gx", "gy", None, None),
        P("gx", "gy", None, None),
        P("gx", "gy", None),
        P("gx", "gy", None, None),
        P("gx", "gy", None),
        P("gx", "gy", None, None),
        P(),
    )
    return jax.shard_map(
        shards, mesh=mesh, in_specs=placed, out_specs=P("gx", "gy", None, None), check_vma=False
    )
```

profile of v0, /device:TPU:7, one launch (start us, length us, event | category | flops | bytes accessed | tf_op | source)
XLA Modules:
  0.0 126.4 jit_solution(14822240542024989627)
XLA Ops:
  7.2 11.3 %all-to-all-start = ((s32[128,2,1]{1,2,0:T(1,128)}), s32[128,2,1]{1,2,0:T(1,128)S(1)}, u32[]{:S(2)}, u32[]{:S(2)}) async-start(s32[128,2,1]{1,2,0:T(1,128)} %bitcast.18), calls=%async_computation | async-start | bytes 131072 | tf_op jit(solution)/shard_map/all_to_all | solution.py:87
  20.0 1.6 %copy.70 = bf16[128,32,32]{1,2,0:T(8,128)(2,1)S(1)} copy(bf16[128,32,32]{0,2,1:T(8,128)(2,1)S(1)} %bitcast.124) | data formatting | bytes 524288 | tf_op jit(solution)/shard_map/reshape;squeeze | solution.py:53
  21.6 2.6 %convolution_multiply_fusion.5 = f32[4,8,64,128]{3,2,1,0:T(8,128)} fusion(bf16[4,8,64,128]{3,2,1,0:T(8,128)(2,1)S(1)} %multiply_convert_fusion, bf16[4,8,9,128,128]{4,3,2,1,0:T(8,128)(2,1)} %param.14, f32[4,8]{1,0:T(4,128)S(1)} %get-tuple-element.10), kind=kOutput, calls=%fused_computation.20 | convolution fusion | flops 67371008 | bytes 2621568 | tf_op jit(solution)/shard_map/abcj,abji->abci/dot_general | solution.py:65
  25.0 1.5 %convolution_convert_fusion.3 = bf16[128,64,32]{1,2,0:T(8,128)(2,1)} fusion(bf16[128,32,32]{1,2,0:T(8,128)(2,1)S(1)} %copy.70, bf16[128,64,32]{1,2,0:T(8,128)(2,1)S(1)} %gather_fusion), kind=kOutput, calls=%fused_computation.10 | convolution fusion | flops 17039360 | bytes 1310720 | tf_op jit(solution)/shard_map/nik,nku->niu/dot_general | solution.py:76
  27.7 1.5 %copy.71 = bf16[128,64,32]{0,2,1:T(8,128)(2,1)S(1)} copy(bf16[128,64,32]{1,2,0:T(8,128)(2,1)S(1)} %copy-done.2) | data formatting | bytes 1048576 | tf_op jit(solution)/shard_map/convert_element_type | solution.py:78
  29.5 1.8 %scatter_custom_fusion.1 = bf16[256,2048]{1,0:T(8,128)(2,1)S(1)} fusion(s32[128]{0:T(128)} %copy-done.17, bf16[128,2048]{1,0:T(8,128)(2,1)S(1)} %copy.72, bf16[]{:T(256)} %constant.3.clone.1), kind=kCustom, calls=%fused_computation.146 | custom fusion | bytes 1049088 | tf_op jit(solution)/shard_map/scatter | solution.py:82
  31.3 1.5 %all_to_all.25 = bf16[128,2,2048]{2,1,0:T(2,128)(2,1)} reshape(bf16[256,2048]{1,0:T(8,128)(2,1)S(1)} %scatter_custom_fusion.1) | data formatting | bytes 2097152 | tf_op jit(solution)/shard_map/all_to_all | solution.py:86
  32.8 9.8 %all-to-all-start.1 = ((bf16[128,2,2048]{2,1,0:T(2,128)(2,1)}), bf16[128,2,2048]{2,1,0:T(2,128)(2,1)S(1)}, u32[]{:S(2)}, u32[]{:S(2)}) async-start(bf16[128,2,2048]{2,1,0:T(2,128)(2,1)} %all_to_all.25), calls=%async_computation.1 | async-start | bytes 2097152 | tf_op jit(solution)/shard_map/all_to_all | solution.py:86
  45.4 1.4 %collective-permute-start.2 = (bf16[6,1,64,128]{3,2,1,0:T(8,128)(2,1)S(1)}, bf16[6,1,64,128]{3,2,1,0:T(8,128)(2,1)S(1)}, u32[]{:S(2)}, u32[]{:S(2)}) collective-permute-start(bf16[6,1,64,128]{3,2,1,0:T(8,128)(2,1)S(1)} %get-tuple-element.16), channel_id=1, source_target_pairs={{0,1},{1,2},{2,3},{3,4},{4,5},{5,6},{6,7},{7,0},{8,9},{9,10},{10,1... | collective-permute-start | bytes 294920 | tf_op jit(solution)/shard_map/ppermute | solution.py:16
  46.8 1.7 %convolution_multiply_fusion.2 = f32[4,8,64,128]{3,2,1,0:T(8,128)S(1)} fusion(bf16[4,8,9,128,128]{4,3,2,1,0:T(8,128)(2,1)} %param.14, bf16[1,8,64,128]{3,2,1,0:T(8,128)(2,1)} %collective-permute-done.1, bf16[4,8,64,128]{3,2,1,0:T(8,128)(2,1)S(1)} %multiply_convert_fusion, f32[4,8]{1,0:T(4,128)S(1)} %copy-done.13), kind=kOutput, calls=%fused_computation.15 | convolution fusion | flops 68681728 | bytes 2752640 | tf_op jit(solution)/shard_map/abcj,abji->abci/dot_general | solution.py:65
  48.5 1.8 %convolution_multiply_fusion.3 = f32[4,8,64,128]{3,2,1,0:T(8,128)S(1)} fusion(bf16[4,8,9,128,128]{4,3,2,1,0:T(8,128)(2,1)} %param.14, bf16[4,8,64,128]{3,2,1,0:T(8,128)(2,1)S(1)} %multiply_convert_fusion, bf16[1,8,64,128]{3,2,1,0:T(8,128)(2,1)} %collective-permute-done, f32[4,8]{1,0:T(4,128)S(1)} %copy-done.15), kind=kOutput, calls=%fused_computation.16 | convolution fusion | flops 68681728 | bytes 2752640 | tf_op jit(solution)/shard_map/abcj,abji->abci/dot_general | solution.py:65
  50.4 7.3 %collective-permute-done.3 = bf16[6,1,64,128]{3,2,1,0:T(8,128)(2,1)S(1)} collective-permute-done((bf16[6,1,64,128]{3,2,1,0:T(8,128)(2,1)S(1)}, bf16[6,1,64,128]{3,2,1,0:T(8,128)(2,1)S(1)}, u32[]{:S(2)}, u32[]{:S(2)}) %collective-permute-start.3) | collective-permute-done | bytes 98336 | tf_op jit(solution)/shard_map/ppermute | solution.py:18
  57.7 1.8 %convolution_multiply_fusion.14 = f32[4,8,64,128]{3,2,1,0:T(8,128)S(1)} fusion(bf16[4,8,9,128,128]{4,3,2,1,0:T(8,128)(2,1)} %param.14, f32[4,8]{1,0:T(4,128)S(1)} %get-tuple-element.9, bf16[6,1,64,128]{3,2,1,0:T(8,128)(2,1)S(1)} %collective-permute-done.3, bf16[1,8,64,128]{3,2,1,0:T(8,128)(2,1)} %collective-permute-done.1, ...), kind=kOutput, calls=%fused_computation.29 | convolution fusion | flops 70909952 | bytes 2982016 | tf_op jit(solution)/shard_map/abcj,abji->abci/dot_general | solution.py:65
  64.6 1.5 %convolution_multiply_fusion.12 = f32[4,8,64,128]{3,2,1,0:T(8,128)S(1)} fusion(bf16[4,8,9,128,128]{4,3,2,1,0:T(8,128)(2,1)S(1)} %bitcast.126, f32[4,8]{1,0:T(4,128)S(1)} %get-tuple-element.6, bf16[6,1,64,128]{3,2,1,0:T(8,128)(2,1)S(1)} %collective-permute-done.3, bf16[1,8,64,128]{3,2,1,0:T(8,128)(2,1)} %collective-permute-done.1, ...), kind=kOutput, calls=%fused_computation.27 | convolution fusion | flops 70909952 | bytes 2983936 | tf_op jit(solution)/shard_map/abcj,abji->abci/dot_general | solution.py:65
  66.1 2.6 %fusion.15 = f32[4,8,64,128]{3,2,1,0:T(8,128)} fusion(f32[4,8,64,128]{3,2,1,0:T(8,128)S(1)} %copy-done.3, f32[4,8,64,128]{3,2,1,0:T(8,128)S(1)} %convolution_multiply_fusion.12, f32[4,8,64,128]{3,2,1,0:T(8,128)S(1)} %convolution_multiply_fusion.2, f32[4,8,64,128]{3,2,1,0:T(8,128)S(1)} %convolution_multiply_fusion.13, ...), kind=kOutput, calls=%fused_computation.48 | convolution fusion | flops 73269248 | bytes 12421120 | tf_op jit(solution)/shard_map/abcj,abji->abci/dot_general | solution.py:65
  69.9 1.7 %convolution_convert_fusion.1 = bf16[32,2048]{1,0:T(8,128)(2,1)S(1)} fusion(bf16[256,2048]{1,0:T(8,128)(2,1)} %all_to_all.27, s32[256]{0:T(256)S(1)} %eq.20), kind=kOutput, calls=%fused_computation.6 | convolution fusion | flops 33628160 | bytes 1180672 | tf_op jit(solution)/shard_map/sk,sf->kf/dot_general | solution.py:92
  72.4 2.4 %fusion.21 = bf16[4,8,64,128]{3,2,1,0:T(8,128)(2,1)S(1)} fusion(f32[4,8,64,128]{3,2,1,0:T(8,128)S(1)} %get-tuple-element.23, f32[4,8,128]{2,1,0:T(8,128)S(1)} %fusion.99, u8[4,64,128]{2,1,0:T(8,128)(4,1)S(1)} %get-tuple-element.22), kind=kLoop, calls=%fused_computation.56 | loop fusion | flops 18087936 | bytes 1622016 | tf_op jit(solution)/shard_map/convert_element_type | solution.py:99
  75.5 2.6 %convolution_multiply_fusion.4 = f32[4,8,64,128]{3,2,1,0:T(8,128)} fusion(bf16[4,8,64,128]{3,2,1,0:T(8,128)(2,1)S(1)} %fusion.21, bf16[4,8,9,128,128]{4,3,2,1,0:T(8,128)(2,1)} %param.14, f32[4,8]{1,0:T(4,128)S(1)} %get-tuple-element.10), kind=kOutput, calls=%fused_computation.18 | convolution fusion | flops 67371008 | bytes 2621568 | tf_op jit(solution)/shard_map/abcj,abji->abci/dot_general | solution.py:65
  78.6 1.5 %collective-permute-start.5 = (bf16[1,8,64,128]{3,2,1,0:T(8,128)(2,1)}, bf16[1,8,64,128]{3,2,1,0:T(8,128)(2,1)}, u32[]{:S(2)}, u32[]{:S(2)}) collective-permute-start(bf16[1,8,64,128]{3,2,1,0:T(8,128)(2,1)} %get-tuple-element.19), channel_id=1, source_target_pairs={{8,0},{16,8},{24,16},{32,24},{40,32},{48,40},{56,48},{64,56},{72,6... | collective-permute-start | bytes 393224 | tf_op jit(solution)/shard_map/ppermute | solution.py:18
  80.8 1.5 %convolution_convert_fusion.2 = bf16[128,64,32]{1,2,0:T(8,128)(2,1)} fusion(bf16[128,32,32]{1,2,0:T(8,128)(2,1)S(1)} %copy.70, bf16[128,64,32]{1,2,0:T(8,128)(2,1)S(1)} %gather_fusion.1), kind=kOutput, calls=%fused_computation.9 | convolution fusion | flops 17039360 | bytes 1310720 | tf_op jit(solution)/shard_map/nik,nku->niu/dot_general | solution.py:76
  83.5 1.5 %copy.75 = bf16[128,64,32]{0,2,1:T(8,128)(2,1)S(1)} copy(bf16[128,64,32]{1,2,0:T(8,128)(2,1)S(1)} %copy-done.1) | data formatting | bytes 1048576 | tf_op jit(solution)/shard_map/convert_element_type | solution.py:78
  85.3 1.8 %scatter_custom_fusion.2 = bf16[256,2048]{1,0:T(8,128)(2,1)S(1)} fusion(s32[128]{0:T(128)} %copy-done.17, bf16[128,2048]{1,0:T(8,128)(2,1)S(1)} %copy.76, bf16[]{:T(256)} %constant.3.clone.1), kind=kCustom, calls=%fused_computation.144 | custom fusion | bytes 1049088 | tf_op jit(solution)/shard_map/scatter | solution.py:82
  87.1 1.5 %all_to_all.28 = bf16[128,2,2048]{2,1,0:T(2,128)(2,1)} reshape(bf16[256,2048]{1,0:T(8,128)(2,1)S(1)} %scatter_custom_fusion.2) | data formatting | bytes 2097152 | tf_op jit(solution)/shard_map/all_to_all | solution.py:86
  88.6 8.2 %all-to-all-start.2 = ((bf16[128,2,2048]{2,1,0:T(2,128)(2,1)}), bf16[128,2,2048]{2,1,0:T(2,128)(2,1)S(1)}, u32[]{:S(2)}, u32[]{:S(2)}) async-start(bf16[128,2,2048]{2,1,0:T(2,128)(2,1)} %all_to_all.28), calls=%async_computation.2 | async-start | bytes 2097152 | tf_op jit(solution)/shard_map/all_to_all | solution.py:86
  98.1 1.4 %collective-permute-start.6 = (bf16[6,1,64,128]{3,2,1,0:T(8,128)(2,1)S(1)}, bf16[6,1,64,128]{3,2,1,0:T(8,128)(2,1)S(1)}, u32[]{:S(2)}, u32[]{:S(2)}) collective-permute-start(bf16[6,1,64,128]{3,2,1,0:T(8,128)(2,1)S(1)} %get-tuple-element.14), channel_id=1, source_target_pairs={{0,1},{1,2},{2,3},{3,4},{4,5},{5,6},{6,7},{7,0},{8,9},{9,10},{10,1... | collective-permute-start | bytes 294920 | tf_op jit(solution)/shard_map/ppermute | solution.py:16
  99.5 1.7 %convolution_multiply_fusion.1 = f32[4,8,64,128]{3,2,1,0:T(8,128)S(1)} fusion(bf16[4,8,9,128,128]{4,3,2,1,0:T(8,128)(2,1)} %param.14, bf16[4,8,64,128]{3,2,1,0:T(8,128)(2,1)S(1)} %fusion.21, bf16[1,8,64,128]{3,2,1,0:T(8,128)(2,1)} %collective-permute-done.4, f32[4,8]{1,0:T(4,128)S(1)} %copy-done.15), kind=kOutput, calls=%fused_computation.14 | convolution fusion | flops 68681728 | bytes 2752640 | tf_op jit(solution)/shard_map/abcj,abji->abci/dot_general | solution.py:65
  101.2 1.8 %convolution_multiply_fusion = f32[4,8,64,128]{3,2,1,0:T(8,128)S(1)} fusion(bf16[4,8,9,128,128]{4,3,2,1,0:T(8,128)(2,1)} %param.14, bf16[1,8,64,128]{3,2,1,0:T(8,128)(2,1)} %collective-permute-done.5, bf16[4,8,64,128]{3,2,1,0:T(8,128)(2,1)S(1)} %fusion.21, f32[4,8]{1,0:T(4,128)S(1)} %copy-done.14), kind=kOutput, calls=%fused_computation.13 | convolution fusion | flops 68681728 | bytes 2752640 | tf_op jit(solution)/shard_map/abcj,abji->abci/dot_general | solution.py:65
  103.1 8.5 %collective-permute-done.7 = bf16[6,1,64,128]{3,2,1,0:T(8,128)(2,1)S(1)} collective-permute-done((bf16[6,1,64,128]{3,2,1,0:T(8,128)(2,1)S(1)}, bf16[6,1,64,128]{3,2,1,0:T(8,128)(2,1)S(1)}, u32[]{:S(2)}, u32[]{:S(2)}) %collective-permute-start.7) | collective-permute-done | bytes 98336 | tf_op jit(solution)/shard_map/ppermute | solution.py:18
  111.6 1.8 %convolution_multiply_fusion.10 = f32[4,8,64,128]{3,2,1,0:T(8,128)S(1)} fusion(bf16[4,8,9,128,128]{4,3,2,1,0:T(8,128)(2,1)} %param.14, f32[4,8]{1,0:T(4,128)S(1)} %get-tuple-element.12, bf16[6,1,64,128]{3,2,1,0:T(8,128)(2,1)S(1)} %collective-permute-done.7, bf16[1,8,64,128]{3,2,1,0:T(8,128)(2,1)} %collective-permute-done.5, ...), kind=kOutput, calls=%fused_computation.25 | convolution fusion | flops 70909952 | bytes 2982016 | tf_op jit(solution)/shard_map/abcj,abji->abci/dot_general | solution.py:65
  117.4 1.4 %convolution_multiply_fusion.6 = f32[4,8,64,128]{3,2,1,0:T(8,128)S(1)} fusion(bf16[4,8,9,128,128]{4,3,2,1,0:T(8,128)(2,1)S(1)} %bitcast.128, f32[4,8]{1,0:T(4,128)S(1)} %get-tuple-element.6, bf16[6,1,64,128]{3,2,1,0:T(8,128)(2,1)S(1)} %collective-permute-done.7, bf16[1,8,64,128]{3,2,1,0:T(8,128)(2,1)} %collective-permute-done.5, ...), kind=kOutput, calls=%fused_computation.21 | convolution fusion | flops 70909952 | bytes 2983936 | tf_op jit(solution)/shard_map/abcj,abji->abci/dot_general | solution.py:65
  118.8 2.6 %fusion.17 = f32[4,8,64,128]{3,2,1,0:T(8,128)} fusion(f32[4,8,64,128]{3,2,1,0:T(8,128)S(1)} %convolution_bitcast_fusion, f32[4,8,64,128]{3,2,1,0:T(8,128)S(1)} %convolution_multiply_fusion.6, f32[4,8,64,128]{3,2,1,0:T(8,128)S(1)} %convolution_multiply_fusion, f32[4,8,64,128]{3,2,1,0:T(8,128)S(1)} %convolution_multiply_fusion.7, ...), kind=kOutput, calls=%fused_computation.50 | convolution fusion | flops 73269248 | bytes 12421120 | tf_op jit(solution)/shard_map/abcj,abji->abci/dot_general | solution.py:65
  123.1 3.3 %fusion.25 = bf16[4,8,64,128]{3,2,1,0:T(8,128)(2,1)} fusion(f32[4,8,64,128]{3,2,1,0:T(8,128)S(1)} %copy-done.18, bf16[4,8,64,32]{3,2,1,0:T(8,128)(2,1)S(1)} %reshape.102, bf16[4,8,32,128]{3,2,1,0:T(8,128)(2,1)S(1)} %copy-done, f32[4,8,128]{2,1,0:T(8,128)S(1)} %fusion.99), kind=kOutput, calls=%fused_computation.60 | convolution fusion | flops 34340864 | bytes 1982464 | tf_op jit(solution)/shard_map/abcr,abrp->abcp/dot_general | solution.py:94
  (106 shorter events, 30.7 us)
Async XLA Ops:
  0.0 72.0 %copy-start = (bf16[4,8,32,128]{3,2,1,0:T(8,128)(2,1)S(1)}, bf16[4,8,32,128]{3,2,1,0:T(8,128)(2,1)}, u32[]{:S(2)}) copy-start(bf16[4,8,32,128]{3,2,1,0:T(8,128)(2,1)} %param.16) | copy-start | bytes 786436
  0.0 5.2 %copy-start.12 = (s32[1,1,128,1]{2,3,1,0:T(1,128)S(1)}, s32[1,1,128,1]{2,3,1,0:T(1,128)}, u32[]{:S(2)}) copy-start(s32[1,1,128,1]{2,3,1,0:T(1,128)} %param.18) | copy-start | bytes 1540
  0.0 18.6 %copy-start.11 = (s32[4,8,9]{2,1,0:T(8,128)S(1)}, s32[4,8,9]{2,1,0:T(8,128)}, u32[]{:S(2)}) copy-start(s32[4,8,9]{2,1,0:T(8,128)} %param.13) | copy-start | bytes 3460
  0.0 19.4 %copy-start.7 = (bf16[4,8,32,128]{3,2,1,0:T(8,128)(2,1)S(1)}, bf16[4,8,32,128]{3,2,1,0:T(8,128)(2,1)}, u32[]{:S(2)}) copy-start(bf16[4,8,32,128]{3,2,1,0:T(8,128)(2,1)} %param.15) | copy-start | bytes 786436
  0.0 19.7 %copy-start.16 = (s32[1,1,128]{2,1,0:T(1,128)S(1)}, s32[1,1,128]{2,1,0:T(1,128)}, u32[]{:S(2)}) copy-start(s32[1,1,128]{2,1,0:T(1,128)} %param.17) | copy-start | bytes 1540
  0.0 19.8 %copy-start.9 = (bf16[1,1,128,1024]{3,2,1,0:T(8,128)(2,1)S(1)}, bf16[1,1,128,1024]{3,2,1,0:T(8,128)(2,1)}, u32[]{:S(2)}) copy-start(bf16[1,1,128,1024]{3,2,1,0:T(8,128)(2,1)} %param.20) | copy-start | bytes 786436
  2.8 41.4 %collective-permute-start = (bf16[1,8,64,128]{3,2,1,0:T(8,128)(2,1)}, bf16[1,8,64,128]{3,2,1,0:T(8,128)(2,1)}, u32[]{:S(2)}, u32[]{:S(2)}) collective-permute-start(bf16[1,8,64,128]{3,2,1,0:T(8,128)(2,1)} %get-tuple-element.20), channel_id=1, source_target_pairs={{0,8},{8,16},{16,24},{24,32},{32,40},{40,48},{48,56},{56,64},{64,7... | collective-permute-start | bytes 393224 | tf_op jit(solution)/shard_map/ppermute | solution.py:16
  4.0 40.2 %collective-permute-start.1 = (bf16[1,8,64,128]{3,2,1,0:T(8,128)(2,1)}, bf16[1,8,64,128]{3,2,1,0:T(8,128)(2,1)}, u32[]{:S(2)}, u32[]{:S(2)}) collective-permute-start(bf16[1,8,64,128]{3,2,1,0:T(8,128)(2,1)} %get-tuple-element.21), channel_id=1, source_target_pairs={{8,0},{16,8},{24,16},{32,24},{40,32},{48,40},{56,48},{64,56},{72,6... | collective-permute-start | bytes 393224 | tf_op jit(solution)/shard_map/ppermute | solution.py:18
  5.3 14.0 %copy-start.17 = (s32[128]{0:T(128)}, s32[128]{0:T(128)S(1)}, u32[]{:S(2)}) copy-start(s32[128]{0:T(128)S(1)} %fusion.100) | copy-start | bytes 1540
  7.2 25.6 %all-to-all-start = ((s32[128,2,1]{1,2,0:T(1,128)}), s32[128,2,1]{1,2,0:T(1,128)S(1)}, u32[]{:S(2)}, u32[]{:S(2)}) async-start(s32[128,2,1]{1,2,0:T(1,128)} %bitcast.18), calls=%async_computation | async-start | bytes 131072 | tf_op jit(solution)/shard_map/all_to_all | solution.py:87
  25.0 1.5 %copy-start.10 = (bf16[2,64,64]{2,1,0:T(8,128)(2,1)S(1)}, bf16[2,64,64]{2,1,0:T(8,128)(2,1)}, u32[]{:S(2)}) copy-start(bf16[2,64,64]{2,1,0:T(8,128)(2,1)} %param.21) | copy-start | bytes 49156
  32.8 14.0 %copy-start.13 = (f32[4,8]{1,0:T(4,128)S(1)}, f32[4,8]{1,0:T(4,128)}, u32[]{:S(2)}) copy-start(f32[4,8]{1,0:T(4,128)} %get-tuple-element.7) | copy-start | bytes 388
  32.8 35.9 %all-to-all-start.1 = ((bf16[128,2,2048]{2,1,0:T(2,128)(2,1)}), bf16[128,2,2048]{2,1,0:T(2,128)(2,1)S(1)}, u32[]{:S(2)}, u32[]{:S(2)}) async-start(bf16[128,2,2048]{2,1,0:T(2,128)(2,1)} %all_to_all.25), calls=%async_computation.1 | async-start | bytes 2097152 | tf_op jit(solution)/shard_map/all_to_all | solution.py:86
  45.0 12.6 %collective-permute-start.3 = (bf16[6,1,64,128]{3,2,1,0:T(8,128)(2,1)S(1)}, bf16[6,1,64,128]{3,2,1,0:T(8,128)(2,1)S(1)}, u32[]{:S(2)}, u32[]{:S(2)}) collective-permute-start(bf16[6,1,64,128]{3,2,1,0:T(8,128)(2,1)S(1)} %get-tuple-element.17), channel_id=1, source_target_pairs={{1,0},{2,1},{3,2},{4,3},{5,4},{6,5},{7,6},{0,7},{9,8},{10,9},{11,1... | collective-permute-start | bytes 294920 | tf_op jit(solution)/shard_map/ppermute | solution.py:18
  45.4 16.5 %collective-permute-start.2 = (bf16[6,1,64,128]{3,2,1,0:T(8,128)(2,1)S(1)}, bf16[6,1,64,128]{3,2,1,0:T(8,128)(2,1)S(1)}, u32[]{:S(2)}, u32[]{:S(2)}) collective-permute-start(bf16[6,1,64,128]{3,2,1,0:T(8,128)(2,1)S(1)} %get-tuple-element.16), channel_id=1, source_target_pairs={{0,1},{1,2},{2,3},{3,4},{4,5},{5,6},{6,7},{7,0},{8,9},{9,10},{10,1... | collective-permute-start | bytes 294920 | tf_op jit(solution)/shard_map/ppermute | solution.py:16
  46.8 1.7 %copy-start.15 = (f32[4,8]{1,0:T(4,128)S(1)}, f32[4,8]{1,0:T(4,128)}, u32[]{:S(2)}) copy-start(f32[4,8]{1,0:T(4,128)} %get-tuple-element.13) | copy-start | bytes 388
  48.5 11.0 %slice-start = ((s8[9437184]{0:T(1024)(128)(4,1)}), s8[4194304]{0:T(1024)(128)(4,1)S(1)}, s32[]{:S(2)}) async-start(s8[9437184]{0:T(1024)(128)(4,1)} %bitcast.125), calls=%async_computation.3 | async-start | bytes 8388608
  57.7 2.6 %slice-start.1 = ((s8[9437184]{0:T(1024)(128)(4,1)}), s8[4194304]{0:T(1024)(128)(4,1)S(1)}, s32[]{:S(2)}) async-start(s8[9437184]{0:T(1024)(128)(4,1)} %bitcast.125), calls=%async_computation.4 | async-start | bytes 8388608
  57.7 2.9 %slice-start.2 = ((s8[9437184]{0:T(1024)(128)(4,1)}), s8[1048576]{0:T(1024)(128)(4,1)S(1)}, s32[]{:S(2)}) async-start(s8[9437184]{0:T(1024)(128)(4,1)} %bitcast.125), calls=%async_computation.5 | async-start | bytes 2097152
  64.5 1.5 %copy-start.3 = (f32[4,8,64,128]{3,2,1,0:T(8,128)S(1)}, f32[4,8,64,128]{3,2,1,0:T(8,128)}, u32[]{:S(2)}) copy-start(f32[4,8,64,128]{3,2,1,0:T(8,128)} %convolution_bitcast_fusion.1) | copy-start | bytes 3145732
  64.6 1.6 %copy-start.5 = (f32[4,8,64,128]{3,2,1,0:T(8,128)S(1)}, f32[4,8,64,128]{3,2,1,0:T(8,128)}, u32[]{:S(2)}) copy-start(f32[4,8,64,128]{3,2,1,0:T(8,128)} %convolution_multiply_fusion.5) | copy-start | bytes 3145732
  69.9 2.1 %copy-start.6 = (f32[4,8,64,128]{3,2,1,0:T(8,128)S(1)}, f32[4,8,64,128]{3,2,1,0:T(8,128)}, u32[]{:S(2)}) copy-start(f32[4,8,64,128]{3,2,1,0:T(8,128)} %fusion.15) | copy-start | bytes 3145732
  74.8 3.3 %copy-start.8 = (bf16[4,8,32,128]{3,2,1,0:T(8,128)(2,1)S(1)}, bf16[4,8,32,128]{3,2,1,0:T(8,128)(2,1)}, u32[]{:S(2)}) copy-start(bf16[4,8,32,128]{3,2,1,0:T(8,128)(2,1)} %param.15) | copy-start | bytes 786436
  78.5 18.4 %collective-permute-start.4 = (bf16[1,8,64,128]{3,2,1,0:T(8,128)(2,1)}, bf16[1,8,64,128]{3,2,1,0:T(8,128)(2,1)}, u32[]{:S(2)}, u32[]{:S(2)}) collective-permute-start(bf16[1,8,64,128]{3,2,1,0:T(8,128)(2,1)} %get-tuple-element.18), channel_id=1, source_target_pairs={{0,8},{8,16},{16,24},{24,32},{32,40},{40,48},{48,56},{56,64},{64,7... | collective-permute-start | bytes 393224 | tf_op jit(solution)/shard_map/ppermute | solution.py:16
  78.6 18.3 %collective-permute-start.5 = (bf16[1,8,64,128]{3,2,1,0:T(8,128)(2,1)}, bf16[1,8,64,128]{3,2,1,0:T(8,128)(2,1)}, u32[]{:S(2)}, u32[]{:S(2)}) collective-permute-start(bf16[1,8,64,128]{3,2,1,0:T(8,128)(2,1)} %get-tuple-element.19), channel_id=1, source_target_pairs={{8,0},{16,8},{24,16},{32,24},{40,32},{48,40},{56,48},{64,56},{72,6... | collective-permute-start | bytes 393224 | tf_op jit(solution)/shard_map/ppermute | solution.py:18
  88.6 32.8 %all-to-all-start.2 = ((bf16[128,2,2048]{2,1,0:T(2,128)(2,1)}), bf16[128,2,2048]{2,1,0:T(2,128)(2,1)S(1)}, u32[]{:S(2)}, u32[]{:S(2)}) async-start(bf16[128,2,2048]{2,1,0:T(2,128)(2,1)} %all_to_all.28), calls=%async_computation.2 | async-start | bytes 2097152 | tf_op jit(solution)/shard_map/all_to_all | solution.py:86
  97.7 13.9 %collective-permute-start.7 = (bf16[6,1,64,128]{3,2,1,0:T(8,128)(2,1)S(1)}, bf16[6,1,64,128]{3,2,1,0:T(8,128)(2,1)S(1)}, u32[]{:S(2)}, u32[]{:S(2)}) collective-permute-start(bf16[6,1,64,128]{3,2,1,0:T(8,128)(2,1)S(1)} %get-tuple-element.15), channel_id=1, source_target_pairs={{1,0},{2,1},{3,2},{4,3},{5,4},{6,5},{7,6},{0,7},{9,8},{10,9},{11,1... | collective-permute-start | bytes 294920 | tf_op jit(solution)/shard_map/ppermute | solution.py:18
  98.1 3.1 %copy-start.14 = (f32[4,8]{1,0:T(4,128)S(1)}, f32[4,8]{1,0:T(4,128)}, u32[]{:S(2)}) copy-start(f32[4,8]{1,0:T(4,128)} %get-tuple-element.7) | copy-start | bytes 388
  98.1 16.7 %collective-permute-start.6 = (bf16[6,1,64,128]{3,2,1,0:T(8,128)(2,1)S(1)}, bf16[6,1,64,128]{3,2,1,0:T(8,128)(2,1)S(1)}, u32[]{:S(2)}, u32[]{:S(2)}) collective-permute-start(bf16[6,1,64,128]{3,2,1,0:T(8,128)(2,1)S(1)} %get-tuple-element.14), channel_id=1, source_target_pairs={{0,1},{1,2},{2,3},{3,4},{4,5},{5,6},{6,7},{7,0},{8,9},{9,10},{10,1... | collective-permute-start | bytes 294920 | tf_op jit(solution)/shard_map/ppermute | solution.py:16
  101.2 12.2 %slice-start.3 = ((s8[9437184]{0:T(1024)(128)(4,1)}), s8[4194304]{0:T(1024)(128)(4,1)S(1)}, s32[]{:S(2)}) async-start(s8[9437184]{0:T(1024)(128)(4,1)} %bitcast.127), calls=%async_computation.6 | async-start | bytes 8388608
  103.0 10.3 %slice-start.4 = ((s8[9437184]{0:T(1024)(128)(4,1)}), s8[4194304]{0:T(1024)(128)(4,1)S(1)}, s32[]{:S(2)}) async-start(s8[9437184]{0:T(1024)(128)(4,1)} %bitcast.127), calls=%async_computation.7 | async-start | bytes 8388608
  103.1 10.3 %slice-start.5 = ((s8[9437184]{0:T(1024)(128)(4,1)}), s8[1048576]{0:T(1024)(128)(4,1)S(1)}, s32[]{:S(2)}) async-start(s8[9437184]{0:T(1024)(128)(4,1)} %bitcast.127), calls=%async_computation.8 | async-start | bytes 2097152
  (4 other events, 5.2 us)
where the time goes:
time: 127 us; the launch traced here: 126 us
  matrix products  42.8 us (34%)
  starting transfers between devices  35.9 us (28%)
  local copies, waits for them, and re-layouts  23.3 us (18%)
  waiting for transfers between devices  15.9 us (13%)
  other arithmetic  7.93 us (6%)
    dot_general x18, matrix products, shards(): jnp.einsum('abcj,abji->abci', shifted, near_tiles[:, :, offset], preferre...  31.9 us
    all_to_all x2, starting transfers between devices, shards(): lax.all_to_all(outbox, ('gx', 'gy'), split_axis=0, concat_axis=0, tiled=T...  18 us
    ppermute x4, waiting for transfers between devices, extended(): lax.ppermute(head, axis, [((i + 1) % count, i) for i in range(count)])  15.8 us
    all_to_all x1, starting transfers between devices, shards(): lax.all_to_all(labels, ('gx', 'gy'), split_axis=0, concat_axis=0, tiled=T...  11.3 us
    all_to_all x4, local copies, waits for them, and re-layouts, shards(): lax.all_to_all(outbox, ('gx', 'gy'), split_axis=0, concat_axis=0, tiled=T...  4.67 us
    ppermute x4, starting transfers between devices, extended(): lax.ppermute(tail, axis, [(i, (i + 1) % count) for i in range(count)])  4.06 us
    dot_general x2, matrix products, shards(): jnp.einsum('abcr,abrp->abcp', gathered, expand_basis, preferred_element_t...  3.67 us
    scatter x2, local copies, waits for them, and re-layouts, shards(): outbox = jnp.zeros((device_list * capacity, chans * rank), jnp.bfloat16)....  3.66 us
  transfers between devices with their start and end apart: 11, of which 2 were waited for; matrix products, arithmetic and copies ran while one was open for 40% of the time, Pallas kernels for 0%

commit v1 on v0

--- a/solution.py
+++ b/solution.py
@@ -1,9 +1,75 @@
+import functools
+
 import jax
 import jax.numpy as jnp
 from jax import lax
+from jax.experimental import pallas as pl
+from jax.experimental.pallas import tpu as pltpu
 from jax.sharding import PartitionSpec as P
 
 LAYERS = 2
+MESH = pl.DeviceIdType.MESH
+
+
+def exchange_kernel(wide_x, wide_y, box_ref, got_ref, inbox, send_sem, recv_sem, row_sem):
+    a, b = lax.axis_index("gx"), lax.axis_index("gy")
+    me = a * wide_y + b
+    count = wide_x * wide_y
+
+    def along_x(step):
+        return lax.rem(a + step, wide_x), b
+
+    def along_y(step):
+        return a, lax.rem(b + step, wide_y)
+
+    barrier = pltpu.get_barrier_semaphore()
+    for step in range(1, wide_y):
+        pl.semaphore_signal(barrier, inc=1, device_id=along_y(step), device_id_type=MESH)
+    for step in range(1, wide_x):
+        pl.semaphore_signal(barrier, inc=1, device_id=along_x(step), device_id_type=MESH)
+    pl.semaphore_wait(barrier, wide_x + wide_y - 2)
+    for step in range(1, wide_x):
+        pl.semaphore_signal(row_sem, inc=1, device_id=along_x(step), device_id_type=MESH)
+    pl.semaphore_wait(row_sem, wide_x - 1)
+
+    def send(step, carry):
+        other = lax.rem(me + step, count)
+        pltpu.make_async_remote_copy(
+            src_ref=box_ref.at[other],
+            dst_ref=inbox.at[me],
+            send_sem=send_sem,
+            recv_sem=recv_sem,
+            device_id=(other // wide_y, lax.rem(other, wide_y)),
+            device_id_type=MESH,
+        ).start()
+        return carry
+
+    lax.fori_loop(1, count, send, 0)
+    own = pltpu.make_async_copy(box_ref.at[me], inbox.at[me], recv_sem)
+    own.start()
+    pltpu.make_async_copy(box_ref, inbox, recv_sem).wait()
+    rest = pl.ds(0, count - 1)
+    pltpu.make_async_copy(box_ref.at[rest], inbox.at[rest], send_sem).wait()
+    got_ref[...] = inbox[...]
+
+
+def exchange(box):
+    wide_x, wide_y = lax.axis_size("gx"), lax.axis_size("gy")
+    return pl.pallas_call(
+        functools.partial(exchange_kernel, wide_x, wide_y),
+        out_shape=jax.ShapeDtypeStruct(box.shape, box.dtype),
+        in_specs=[pl.BlockSpec(memory_space=pltpu.VMEM)],
+        out_specs=pl.BlockSpec(memory_space=pltpu.VMEM),
+        scratch_shapes=[
+            pltpu.VMEM(box.shape, box.dtype),
+            pltpu.SemaphoreType.DMA,
+            pltpu.SemaphoreType.DMA,
+            pltpu.SemaphoreType.REGULAR,
+        ],
+        compiler_params=pltpu.CompilerParams(
+            collective_id=0, has_side_effects=True, vmem_limit_bytes=32 << 20
+        ),
+    )(box)
 
 
 def extended(cells, sides, width):
@@ -82,9 +148,10 @@
             .set(term.reshape(pairs, chans * rank))
         )
         labels = jnp.zeros((device_list * capacity,), jnp.int32).at[position].set(target_cell)
-        inbox, incoming_labels = (
-            lax.all_to_all(outbox, ("gx", "gy"), split_axis=0, concat_axis=0, tiled=True),
-            lax.all_to_all(labels, ("gx", "gy"), split_axis=0, concat_axis=0, tiled=True),
+        inbox = exchange(outbox.reshape(device_list, capacity * chans * rank // 128, 128))
+        inbox = inbox.reshape(device_list * capacity, chans * rank)
+        incoming_labels = lax.all_to_all(
+            labels, ("gx", "gy"), split_axis=0, concat_axis=0, tiled=True
         )
         selection_mask = (
             incoming_labels[:, None] == jnp.arange(cells, dtype=jnp.int32)[None, :]

time: 127 us -> 142 us (1.12)
  the two profiles are of different devices: /device:TPU:7 before, /device:TPU:1 now
where the time goes in v1:
time: 142 us
  Pallas kernels  48.4 us (34%)
  matrix products  39.7 us (28%)
  local copies, waits for them, and re-layouts  22.6 us (16%)
  starting transfers between devices  22.4 us (16%)
  other arithmetic  7.83 us (6%)
    pallas_call x2, Pallas kernels, exchange(): pl.pallas_call(functools.partial(exchange_kernel, wide_x, wide_y), out_sh...  48.4 us
    dot_general x18, matrix products, shards(): jnp.einsum('abcj,abji->abci', shifted, near_tiles[:, :, offset], preferre...  29.2 us
    ppermute x4, starting transfers between devices, extended(): lax.ppermute(head, axis, [((i + 1) % count, i) for i in range(count)])  9.53 us
    all_to_all x1, starting transfers between devices, shards(): lax.all_to_all(labels, ('gx', 'gy'), split_axis=0, concat_axis=0, tiled=T...  7.76 us
    ppermute x4, starting transfers between devices, extended(): lax.ppermute(tail, axis, [(i, (i + 1) % count) for i in range(count)])  5.08 us
    convert_element_type x2, local copies, waits for them, and re-layouts, shards(): term = jnp.einsum('nik,nku->niu', picked_entries, pair_linkage, preferred...  4.38 us
    scatter x2, local copies, waits for them, and re-layouts, shards(): outbox = jnp.zeros((device_list * capacity, chans * rank), jnp.bfloat16)....  4.06 us
    dot_general x2, matrix products, shards(): jnp.einsum('abcr,abrp->abcp', gathered, expand_basis, preferred_element_t...  3.7 us
  transfers between devices with their start and end apart: 9, of which 0 were waited for; matrix products, arithmetic and copies ran while one was open for 29% of the time, Pallas kernels for 34%

profile of v1, /device:TPU:1, one launch (start us, length us, event | category | flops | bytes accessed | tf_op | source)
XLA Modules:
  0.0 141.6 jit_solution(17469991801559713254)
XLA Ops:
  2.8 2.0 %collective-permute-start = (bf16[1,8,64,128]{3,2,1,0:T(8,128)(2,1)}, bf16[1,8,64,128]{3,2,1,0:T(8,128)(2,1)}, u32[]{:S(2)}, u32[]{:S(2)}) collective-permute-start(bf16[1,8,64,128]{3,2,1,0:T(8,128)(2,1)} %get-tuple-element.20), channel_id=1, source_target_pairs={{0,8},{8,16},{16,24},{24,32},{32,40},{40,48},{48,56},{56,64},{64,7... | collective-permute-start | bytes 393224 | tf_op jit(solution)/shard_map/ppermute | solution.py:82
  4.8 3.7 %collective-permute-start.1 = (bf16[1,8,64,128]{3,2,1,0:T(8,128)(2,1)}, bf16[1,8,64,128]{3,2,1,0:T(8,128)(2,1)}, u32[]{:S(2)}, u32[]{:S(2)}) collective-permute-start(bf16[1,8,64,128]{3,2,1,0:T(8,128)(2,1)} %get-tuple-element.21), channel_id=1, source_target_pairs={{8,0},{16,8},{24,16},{32,24},{40,32},{48,40},{56,48},{64,56},{72,6... | collective-permute-start | bytes 393224 | tf_op jit(solution)/shard_map/ppermute | solution.py:84
  11.5 7.8 %all-to-all-start = ((s32[128,2,1]{1,2,0:T(1,128)}), s32[128,2,1]{1,2,0:T(1,128)S(1)}, u32[]{:S(2)}, u32[]{:S(2)}) async-start(s32[128,2,1]{1,2,0:T(1,128)} %bitcast.18), calls=%async_computation | async-start | bytes 131072 | tf_op jit(solution)/shard_map/all_to_all | solution.py:153
  20.7 1.6 %copy.70 = bf16[128,32,32]{1,2,0:T(8,128)(2,1)S(1)} copy(bf16[128,32,32]{0,2,1:T(8,128)(2,1)S(1)} %bitcast.124) | data formatting | bytes 524288 | tf_op jit(solution)/shard_map/reshape;squeeze | solution.py:119
  22.3 3.0 %convolution_multiply_fusion.5 = f32[4,8,64,128]{3,2,1,0:T(8,128)} fusion(bf16[4,8,64,128]{3,2,1,0:T(8,128)(2,1)S(1)} %multiply_convert_fusion, bf16[4,8,9,128,128]{4,3,2,1,0:T(8,128)(2,1)} %param.14, f32[4,8]{1,0:T(4,128)S(1)} %get-tuple-element.10), kind=kOutput, calls=%fused_computation.20 | convolution fusion | flops 67371008 | bytes 2621568 | tf_op jit(solution)/shard_map/abcj,abji->abci/dot_general | solution.py:131
  26.1 1.4 convolution_convert_fusion.3
  28.8 1.5 %copy.71 = bf16[128,64,32]{0,2,1:T(8,128)(2,1)S(1)} copy(bf16[128,64,32]{1,2,0:T(8,128)(2,1)S(1)} %copy-done.3) | data formatting | bytes 1048576 | tf_op jit(solution)/shard_map/convert_element_type | solution.py:144
  30.6 2.0 %scatter_custom_fusion.1 = bf16[256,2048]{1,0:T(8,128)(2,1)S(1)} fusion(s32[128]{0:T(128)} %copy-done.17, bf16[128,2048]{1,0:T(8,128)(2,1)S(1)} %copy.72, bf16[]{:T(256)} %constant.3.clone.1), kind=kCustom, calls=%fused_computation.146 | custom fusion | bytes 1049088 | tf_op jit(solution)/shard_map/scatter | solution.py:148
  33.1 25.4 %shard_map.109 = bf16[128,32,128]{2,1,0:T(8,128)(2,1)S(1)} custom-call(bf16[128,32,128]{2,1,0:T(8,128)(2,1)S(1)} %reshape.107.box_ref), custom_call_target="tpu_custom_call" | custom-call | tf_op jit(solution)/shard_map/pallas_call | solution.py:58
  63.8 1.7 %convolution_multiply_fusion.2 = f32[4,8,64,128]{3,2,1,0:T(8,128)S(1)} fusion(bf16[4,8,9,128,128]{4,3,2,1,0:T(8,128)(2,1)} %param.14, bf16[1,8,64,128]{3,2,1,0:T(8,128)(2,1)} %collective-permute-done.1, bf16[4,8,64,128]{3,2,1,0:T(8,128)(2,1)S(1)} %multiply_convert_fusion, f32[4,8]{1,0:T(4,128)S(1)} %copy-done.13), kind=kOutput, calls=%fused_computation.15 | convolution fusion | flops 68681728 | bytes 2752640 | tf_op jit(solution)/shard_map/abcj,abji->abci/dot_general | solution.py:131
  65.6 1.8 %convolution_multiply_fusion.3 = f32[4,8,64,128]{3,2,1,0:T(8,128)S(1)} fusion(bf16[4,8,9,128,128]{4,3,2,1,0:T(8,128)(2,1)} %param.14, bf16[4,8,64,128]{3,2,1,0:T(8,128)(2,1)S(1)} %multiply_convert_fusion, bf16[1,8,64,128]{3,2,1,0:T(8,128)(2,1)} %collective-permute-done, f32[4,8]{1,0:T(4,128)S(1)} %copy-done.15), kind=kOutput, calls=%fused_computation.16 | convolution fusion | flops 68681728 | bytes 2752640 | tf_op jit(solution)/shard_map/abcj,abji->abci/dot_general | solution.py:131
  67.5 1.8 %convolution_multiply_fusion.14 = f32[4,8,64,128]{3,2,1,0:T(8,128)S(1)} fusion(bf16[4,8,9,128,128]{4,3,2,1,0:T(8,128)(2,1)} %param.14, f32[4,8]{1,0:T(4,128)S(1)} %get-tuple-element.9, bf16[6,1,64,128]{3,2,1,0:T(8,128)(2,1)S(1)} %collective-permute-done.3, bf16[1,8,64,128]{3,2,1,0:T(8,128)(2,1)} %collective-permute-done.1, ...), kind=kOutput, calls=%fused_computation.29 | convolution fusion | flops 70909952 | bytes 2982016 | tf_op jit(solution)/shard_map/abcj,abji->abci/dot_general | solution.py:131
  70.4 1.4 convolution_multiply_fusion.16
  71.8 1.3 convolution_multiply_fusion.15
  73.1 1.3 convolution_multiply_fusion.13
  74.4 1.5 %convolution_multiply_fusion.12 = f32[4,8,64,128]{3,2,1,0:T(8,128)S(1)} fusion(bf16[4,8,9,128,128]{4,3,2,1,0:T(8,128)(2,1)S(1)} %bitcast.126, f32[4,8]{1,0:T(4,128)S(1)} %get-tuple-element.6, bf16[6,1,64,128]{3,2,1,0:T(8,128)(2,1)S(1)} %collective-permute-done.3, bf16[1,8,64,128]{3,2,1,0:T(8,128)(2,1)} %collective-permute-done.1, ...), kind=kOutput, calls=%fused_computation.27 | convolution fusion | flops 70909952 | bytes 2983936 | tf_op jit(solution)/shard_map/abcj,abji->abci/dot_general | solution.py:131
  76.0 1.6 %fusion.15 = f32[4,8,64,128]{3,2,1,0:T(8,128)S(1)} fusion(f32[4,8,64,128]{3,2,1,0:T(8,128)S(1)} %copy-done.5, f32[4,8,64,128]{3,2,1,0:T(8,128)S(1)} %convolution_multiply_fusion.12, f32[4,8,64,128]{3,2,1,0:T(8,128)S(1)} %convolution_multiply_fusion.2, f32[4,8,64,128]{3,2,1,0:T(8,128)S(1)} %convolution_multiply_fusion.13, ...), kind=kOutput, calls=%fused_computation.48 | convolution fusion | flops 73269248 | bytes 12421120 | tf_op jit(solution)/shard_map/abcj,abji->abci/dot_general | solution.py:131
  78.0 2.4 %fusion.21 = bf16[4,8,64,128]{3,2,1,0:T(8,128)(2,1)S(1)} fusion(f32[4,8,64,128]{3,2,1,0:T(8,128)S(1)} %get-tuple-element.23, f32[4,8,128]{2,1,0:T(8,128)S(1)} %fusion.99, u8[4,64,128]{2,1,0:T(8,128)(4,1)S(1)} %get-tuple-element.22), kind=kLoop, calls=%fused_computation.56 | loop fusion | flops 18087936 | bytes 1622016 | tf_op jit(solution)/shard_map/convert_element_type | solution.py:166
  81.1 1.4 %convolution_multiply_fusion.4 = f32[4,8,64,128]{3,2,1,0:T(8,128)} fusion(bf16[4,8,64,128]{3,2,1,0:T(8,128)(2,1)S(1)} %fusion.21, bf16[4,8,9,128,128]{4,3,2,1,0:T(8,128)(2,1)S(1)} %bitcast.126, f32[4,8]{1,0:T(4,128)S(1)} %get-tuple-element.10), kind=kOutput, calls=%fused_computation.18 | convolution fusion | flops 67371008 | bytes 2623488 | tf_op jit(solution)/shard_map/abcj,abji->abci/dot_general | solution.py:131
  84.4 4.7 %collective-permute-start.5 = (bf16[1,8,64,128]{3,2,1,0:T(8,128)(2,1)}, bf16[1,8,64,128]{3,2,1,0:T(8,128)(2,1)}, u32[]{:S(2)}, u32[]{:S(2)}) collective-permute-start(bf16[1,8,64,128]{3,2,1,0:T(8,128)(2,1)} %get-tuple-element.19), channel_id=1, source_target_pairs={{8,0},{16,8},{24,16},{32,24},{40,32},{48,40},{56,48},{64,56},{72,6... | collective-permute-start | bytes 393224 | tf_op jit(solution)/shard_map/ppermute | solution.py:84
  90.3 1.4 convolution_convert_fusion.2
  91.7 2.8 %copy.75 = bf16[128,64,32]{0,2,1:T(8,128)(2,1)S(1)} copy(bf16[128,64,32]{1,2,0:T(8,128)(2,1)} %convolution_convert_fusion.2) | data formatting | bytes 1048576 | tf_op jit(solution)/shard_map/convert_element_type | solution.py:144
  94.7 2.0 %scatter_custom_fusion.2 = bf16[256,2048]{1,0:T(8,128)(2,1)S(1)} fusion(s32[128]{0:T(128)} %copy-done.17, bf16[128,2048]{1,0:T(8,128)(2,1)S(1)} %copy.76, bf16[]{:T(256)} %constant.3.clone.1), kind=kCustom, calls=%fused_computation.144 | custom fusion | bytes 1049088 | tf_op jit(solution)/shard_map/scatter | solution.py:148
  97.3 23.1 %shard_map.110 = bf16[128,32,128]{2,1,0:T(8,128)(2,1)S(1)} custom-call(bf16[128,32,128]{2,1,0:T(8,128)(2,1)S(1)} %reshape.112.box_ref), custom_call_target="tpu_custom_call" | custom-call | tf_op jit(solution)/shard_map/pallas_call | solution.py:58
  123.0 1.7 %collective-permute-start.6 = (bf16[6,1,64,128]{3,2,1,0:T(8,128)(2,1)S(1)}, bf16[6,1,64,128]{3,2,1,0:T(8,128)(2,1)S(1)}, u32[]{:S(2)}, u32[]{:S(2)}) collective-permute-start(bf16[6,1,64,128]{3,2,1,0:T(8,128)(2,1)S(1)} %get-tuple-element.14), channel_id=1, source_target_pairs={{0,1},{1,2},{2,3},{3,4},{4,5},{5,6},{6,7},{7,0},{8,9},{9,10},{10,1... | collective-permute-start | bytes 294920 | tf_op jit(solution)/shard_map/ppermute | solution.py:82
  124.7 1.6 %convolution_multiply_fusion.1 = f32[4,8,64,128]{3,2,1,0:T(8,128)S(1)} fusion(bf16[4,8,9,128,128]{4,3,2,1,0:T(8,128)(2,1)} %param.14, bf16[4,8,64,128]{3,2,1,0:T(8,128)(2,1)S(1)} %fusion.21, bf16[1,8,64,128]{3,2,1,0:T(8,128)(2,1)S(1)} %collective-permute-done.4, f32[4,8]{1,0:T(4,128)S(1)} %copy-done.15), kind=kOutput, calls=%fused_computation.14 | convolution fusion | flops 68681728 | bytes 2752640 | tf_op jit(solution)/shard_map/abcj,abji->abci/dot_general | solution.py:131
  126.4 1.8 %convolution_multiply_fusion = f32[4,8,64,128]{3,2,1,0:T(8,128)S(1)} fusion(bf16[4,8,9,128,128]{4,3,2,1,0:T(8,128)(2,1)} %param.14, bf16[1,8,64,128]{3,2,1,0:T(8,128)(2,1)} %collective-permute-done.5, bf16[4,8,64,128]{3,2,1,0:T(8,128)(2,1)S(1)} %fusion.21, f32[4,8]{1,0:T(4,128)S(1)} %copy-done.14), kind=kOutput, calls=%fused_computation.13 | convolution fusion | flops 68681728 | bytes 2752640 | tf_op jit(solution)/shard_map/abcj,abji->abci/dot_general | solution.py:131
  128.2 1.8 %convolution_multiply_fusion.10 = f32[4,8,64,128]{3,2,1,0:T(8,128)S(1)} fusion(bf16[4,8,9,128,128]{4,3,2,1,0:T(8,128)(2,1)} %param.14, f32[4,8]{1,0:T(4,128)S(1)} %get-tuple-element.12, bf16[6,1,64,128]{3,2,1,0:T(8,128)(2,1)S(1)} %collective-permute-done.7, bf16[1,8,64,128]{3,2,1,0:T(8,128)(2,1)} %collective-permute-done.5, ...), kind=kOutput, calls=%fused_computation.25 | convolution fusion | flops 70909952 | bytes 2982016 | tf_op jit(solution)/shard_map/abcj,abji->abci/dot_general | solution.py:131
  133.8 1.3 convolution_multiply_fusion.7
  135.2 1.5 %convolution_multiply_fusion.6 = f32[4,8,64,128]{3,2,1,0:T(8,128)S(1)} fusion(bf16[4,8,9,128,128]{4,3,2,1,0:T(8,128)(2,1)S(1)} %bitcast.128, f32[4,8]{1,0:T(4,128)S(1)} %get-tuple-element.6, bf16[6,1,64,128]{3,2,1,0:T(8,128)(2,1)S(1)} %collective-permute-done.7, bf16[1,8,64,128]{3,2,1,0:T(8,128)(2,1)} %collective-permute-done.5, ...), kind=kOutput, calls=%fused_computation.21 | convolution fusion | flops 70909952 | bytes 2983936 | tf_op jit(solution)/shard_map/abcj,abji->abci/dot_general | solution.py:131
  136.7 1.6 %fusion.17 = f32[4,8,64,128]{3,2,1,0:T(8,128)S(1)} fusion(f32[4,8,64,128]{3,2,1,0:T(8,128)S(1)} %copy-done.4, f32[4,8,64,128]{3,2,1,0:T(8,128)S(1)} %convolution_multiply_fusion.6, f32[4,8,64,128]{3,2,1,0:T(8,128)S(1)} %convolution_multiply_fusion, f32[4,8,64,128]{3,2,1,0:T(8,128)S(1)} %convolution_multiply_fusion.7, ...), kind=kOutput, calls=%fused_computation.50 | convolution fusion | flops 73269248 | bytes 12421120 | tf_op jit(solution)/shard_map/abcj,abji->abci/dot_general | solution.py:131
  138.3 3.3 %fusion.25 = bf16[4,8,64,128]{3,2,1,0:T(8,128)(2,1)} fusion(f32[4,8,64,128]{3,2,1,0:T(8,128)S(1)} %fusion.17, bf16[4,8,64,32]{3,2,1,0:T(8,128)(2,1)S(1)} %reshape.114, bf16[4,8,32,128]{3,2,1,0:T(8,128)(2,1)S(1)} %copy-done, f32[4,8,128]{2,1,0:T(8,128)S(1)} %fusion.99), kind=kOutput, calls=%fused_computation.60 | convolution fusion | flops 34340864 | bytes 1982464 | tf_op jit(solution)/shard_map/abcr,abrp->abcp/dot_general | solution.py:161
  (102 shorter events, 27.5 us)
Async XLA Ops:
  0.0 77.6 %copy-start = (bf16[4,8,32,128]{3,2,1,0:T(8,128)(2,1)S(1)}, bf16[4,8,32,128]{3,2,1,0:T(8,128)(2,1)}, u32[]{:S(2)}) copy-start(bf16[4,8,32,128]{3,2,1,0:T(8,128)(2,1)} %param.16) | copy-start | bytes 786436
  0.0 9.4 %copy-start.12 = (s32[1,1,128,1]{2,3,1,0:T(1,128)S(1)}, s32[1,1,128,1]{2,3,1,0:T(1,128)}, u32[]{:S(2)}) copy-start(s32[1,1,128,1]{2,3,1,0:T(1,128)} %param.18) | copy-start | bytes 1540
  0.0 19.3 %copy-start.11 = (s32[4,8,9]{2,1,0:T(8,128)S(1)}, s32[4,8,9]{2,1,0:T(8,128)}, u32[]{:S(2)}) copy-start(s32[4,8,9]{2,1,0:T(8,128)} %param.13) | copy-start | bytes 3460
  0.0 20.1 %copy-start.8 = (bf16[4,8,32,128]{3,2,1,0:T(8,128)(2,1)S(1)}, bf16[4,8,32,128]{3,2,1,0:T(8,128)(2,1)}, u32[]{:S(2)}) copy-start(bf16[4,8,32,128]{3,2,1,0:T(8,128)(2,1)} %param.15) | copy-start | bytes 786436
  0.0 20.4 %copy-start.16 = (s32[1,1,128]{2,1,0:T(1,128)S(1)}, s32[1,1,128]{2,1,0:T(1,128)}, u32[]{:S(2)}) copy-start(s32[1,1,128]{2,1,0:T(1,128)} %param.17) | copy-start | bytes 1540
  0.0 20.5 %copy-start.9 = (bf16[1,1,128,1024]{3,2,1,0:T(8,128)(2,1)S(1)}, bf16[1,1,128,1024]{3,2,1,0:T(8,128)(2,1)}, u32[]{:S(2)}) copy-start(bf16[1,1,128,1024]{3,2,1,0:T(8,128)(2,1)} %param.20) | copy-start | bytes 786436
  2.8 58.5 %collective-permute-start = (bf16[1,8,64,128]{3,2,1,0:T(8,128)(2,1)}, bf16[1,8,64,128]{3,2,1,0:T(8,128)(2,1)}, u32[]{:S(2)}, u32[]{:S(2)}) collective-permute-start(bf16[1,8,64,128]{3,2,1,0:T(8,128)(2,1)} %get-tuple-element.20), channel_id=1, source_target_pairs={{0,8},{8,16},{16,24},{24,32},{32,40},{40,48},{48,56},{56,64},{64,7... | collective-permute-start | bytes 393224 | tf_op jit(solution)/shard_map/ppermute | solution.py:82
  4.8 56.5 %collective-permute-start.1 = (bf16[1,8,64,128]{3,2,1,0:T(8,128)(2,1)}, bf16[1,8,64,128]{3,2,1,0:T(8,128)(2,1)}, u32[]{:S(2)}, u32[]{:S(2)}) collective-permute-start(bf16[1,8,64,128]{3,2,1,0:T(8,128)(2,1)} %get-tuple-element.21), channel_id=1, source_target_pairs={{8,0},{16,8},{24,16},{32,24},{40,32},{48,40},{56,48},{64,56},{72,6... | collective-permute-start | bytes 393224 | tf_op jit(solution)/shard_map/ppermute | solution.py:84
  9.6 10.4 %copy-start.17 = (s32[128]{0:T(128)}, s32[128]{0:T(128)S(1)}, u32[]{:S(2)}) copy-start(s32[128]{0:T(128)S(1)} %fusion.100) | copy-start | bytes 1540
  11.5 47.5 %all-to-all-start = ((s32[128,2,1]{1,2,0:T(1,128)}), s32[128,2,1]{1,2,0:T(1,128)S(1)}, u32[]{:S(2)}, u32[]{:S(2)}) async-start(s32[128,2,1]{1,2,0:T(1,128)} %bitcast.18), calls=%async_computation | async-start | bytes 131072 | tf_op jit(solution)/shard_map/all_to_all | solution.py:153
  22.3 3.8 %copy-start.1 = (bf16[128,32,32]{1,2,0:T(8,128)(2,1)}, bf16[128,32,32]{1,2,0:T(8,128)(2,1)S(1)}, u32[]{:S(2)}) copy-start(bf16[128,32,32]{1,2,0:T(8,128)(2,1)S(1)} %copy.70) | copy-start | bytes 786436
  26.1 1.4 copy-start.10
  27.5 1.3 copy-start.3
  59.0 4.8 %copy-start.13 = (f32[4,8]{1,0:T(4,128)S(1)}, f32[4,8]{1,0:T(4,128)}, u32[]{:S(2)}) copy-start(f32[4,8]{1,0:T(4,128)} %get-tuple-element.7) | copy-start | bytes 388
  62.1 5.4 %collective-permute-start.3 = (bf16[6,1,64,128]{3,2,1,0:T(8,128)(2,1)S(1)}, bf16[6,1,64,128]{3,2,1,0:T(8,128)(2,1)S(1)}, u32[]{:S(2)}, u32[]{:S(2)}) collective-permute-start(bf16[6,1,64,128]{3,2,1,0:T(8,128)(2,1)S(1)} %get-tuple-element.17), channel_id=1, source_target_pairs={{1,0},{2,1},{3,2},{4,3},{5,4},{6,5},{7,6},{0,7},{9,8},{10,9},{11,1... | collective-permute-start | bytes 294920 | tf_op jit(solution)/shard_map/ppermute | solution.py:84
  62.7 9.1 %collective-permute-start.2 = (bf16[6,1,64,128]{3,2,1,0:T(8,128)(2,1)S(1)}, bf16[6,1,64,128]{3,2,1,0:T(8,128)(2,1)S(1)}, u32[]{:S(2)}, u32[]{:S(2)}) collective-permute-start(bf16[6,1,64,128]{3,2,1,0:T(8,128)(2,1)S(1)} %get-tuple-element.16), channel_id=1, source_target_pairs={{0,1},{1,2},{2,3},{3,4},{4,5},{5,6},{6,7},{7,0},{8,9},{9,10},{10,1... | collective-permute-start | bytes 294920 | tf_op jit(solution)/shard_map/ppermute | solution.py:82
  63.8 1.7 %copy-start.15 = (f32[4,8]{1,0:T(4,128)S(1)}, f32[4,8]{1,0:T(4,128)}, u32[]{:S(2)}) copy-start(f32[4,8]{1,0:T(4,128)} %get-tuple-element.13) | copy-start | bytes 388
  65.6 3.7 %slice-start = ((s8[9437184]{0:T(1024)(128)(4,1)}), s8[4194304]{0:T(1024)(128)(4,1)S(1)}, s32[]{:S(2)}) async-start(s8[9437184]{0:T(1024)(128)(4,1)} %bitcast.125), calls=%async_computation.1 | async-start | bytes 8388608
  67.4 2.7 %slice-start.1 = ((s8[9437184]{0:T(1024)(128)(4,1)}), s8[4194304]{0:T(1024)(128)(4,1)S(1)}, s32[]{:S(2)}) async-start(s8[9437184]{0:T(1024)(128)(4,1)} %bitcast.125), calls=%async_computation.2 | async-start | bytes 8388608
  67.4 3.0 %slice-start.2 = ((s8[9437184]{0:T(1024)(128)(4,1)}), s8[1048576]{0:T(1024)(128)(4,1)S(1)}, s32[]{:S(2)}) async-start(s8[9437184]{0:T(1024)(128)(4,1)} %bitcast.125), calls=%async_computation.3 | async-start | bytes 2097152
  74.4 1.5 %copy-start.5 = (f32[4,8,64,128]{3,2,1,0:T(8,128)S(1)}, f32[4,8,64,128]{3,2,1,0:T(8,128)}, u32[]{:S(2)}) copy-start(f32[4,8,64,128]{3,2,1,0:T(8,128)} %convolution_bitcast_fusion.1) | copy-start | bytes 3145732
  74.4 1.6 %copy-start.7 = (f32[4,8,64,128]{3,2,1,0:T(8,128)S(1)}, f32[4,8,64,128]{3,2,1,0:T(8,128)}, u32[]{:S(2)}) copy-start(f32[4,8,64,128]{3,2,1,0:T(8,128)} %convolution_multiply_fusion.5) | copy-start | bytes 3145732
  84.2 37.5 %collective-permute-start.4 = (bf16[1,8,64,128]{3,2,1,0:T(8,128)(2,1)}, bf16[1,8,64,128]{3,2,1,0:T(8,128)(2,1)S(1)}, u32[]{:S(2)}, u32[]{:S(2)}) collective-permute-start(bf16[1,8,64,128]{3,2,1,0:T(8,128)(2,1)} %get-tuple-element.18), channel_id=1, source_target_pairs={{0,8},{8,16},{16,24},{24,32},{32,40},{40,48},{48,56},{56,64},{64,7... | collective-permute-start | bytes 393224 | tf_op jit(solution)/shard_map/ppermute | solution.py:82
  84.4 37.3 %collective-permute-start.5 = (bf16[1,8,64,128]{3,2,1,0:T(8,128)(2,1)}, bf16[1,8,64,128]{3,2,1,0:T(8,128)(2,1)}, u32[]{:S(2)}, u32[]{:S(2)}) collective-permute-start(bf16[1,8,64,128]{3,2,1,0:T(8,128)(2,1)} %get-tuple-element.19), channel_id=1, source_target_pairs={{8,0},{16,8},{24,16},{32,24},{40,32},{48,40},{56,48},{64,56},{72,6... | collective-permute-start | bytes 393224 | tf_op jit(solution)/shard_map/ppermute | solution.py:84
  122.5 5.8 %collective-permute-start.7 = (bf16[6,1,64,128]{3,2,1,0:T(8,128)(2,1)S(1)}, bf16[6,1,64,128]{3,2,1,0:T(8,128)(2,1)S(1)}, u32[]{:S(2)}, u32[]{:S(2)}) collective-permute-start(bf16[6,1,64,128]{3,2,1,0:T(8,128)(2,1)S(1)} %get-tuple-element.15), channel_id=1, source_target_pairs={{1,0},{2,1},{3,2},{4,3},{5,4},{6,5},{7,6},{0,7},{9,8},{10,9},{11,1... | collective-permute-start | bytes 294920 | tf_op jit(solution)/shard_map/ppermute | solution.py:84
  123.0 3.4 %copy-start.14 = (f32[4,8]{1,0:T(4,128)S(1)}, f32[4,8]{1,0:T(4,128)}, u32[]{:S(2)}) copy-start(f32[4,8]{1,0:T(4,128)} %get-tuple-element.7) | copy-start | bytes 388
  123.0 9.5 %collective-permute-start.6 = (bf16[6,1,64,128]{3,2,1,0:T(8,128)(2,1)S(1)}, bf16[6,1,64,128]{3,2,1,0:T(8,128)(2,1)S(1)}, u32[]{:S(2)}, u32[]{:S(2)}) collective-permute-start(bf16[6,1,64,128]{3,2,1,0:T(8,128)(2,1)S(1)} %get-tuple-element.14), channel_id=1, source_target_pairs={{0,1},{1,2},{2,3},{3,4},{4,5},{5,6},{6,7},{7,0},{8,9},{9,10},{10,1... | collective-permute-start | bytes 294920 | tf_op jit(solution)/shard_map/ppermute | solution.py:82
  126.4 3.7 %slice-start.3 = ((s8[9437184]{0:T(1024)(128)(4,1)}), s8[4194304]{0:T(1024)(128)(4,1)S(1)}, s32[]{:S(2)}) async-start(s8[9437184]{0:T(1024)(128)(4,1)} %bitcast.127), calls=%async_computation.4 | async-start | bytes 8388608
  128.2 2.7 %slice-start.4 = ((s8[9437184]{0:T(1024)(128)(4,1)}), s8[4194304]{0:T(1024)(128)(4,1)S(1)}, s32[]{:S(2)}) async-start(s8[9437184]{0:T(1024)(128)(4,1)} %bitcast.127), calls=%async_computation.5 | async-start | bytes 8388608
  128.2 3.0 %slice-start.5 = ((s8[9437184]{0:T(1024)(128)(4,1)}), s8[1048576]{0:T(1024)(128)(4,1)S(1)}, s32[]{:S(2)}) async-start(s8[9437184]{0:T(1024)(128)(4,1)} %bitcast.127), calls=%async_computation.6 | async-start | bytes 2097152
  135.1 1.5 %copy-start.4 = (f32[4,8,64,128]{3,2,1,0:T(8,128)S(1)}, f32[4,8,64,128]{3,2,1,0:T(8,128)}, u32[]{:S(2)}) copy-start(f32[4,8,64,128]{3,2,1,0:T(8,128)} %convolution_bitcast_fusion) | copy-start | bytes 3145732
  135.1 1.6 %copy-start.6 = (f32[4,8,64,128]{3,2,1,0:T(8,128)S(1)}, f32[4,8,64,128]{3,2,1,0:T(8,128)}, u32[]{:S(2)}) copy-start(f32[4,8,64,128]{3,2,1,0:T(8,128)} %convolution_multiply_fusion.4) | copy-start | bytes 3145732
  (1 other events, 1.2 us)

commit v2 on v0

v2 whole, which is shorter than its diff:
```python
import functools

import jax
import jax.numpy as jnp
from jax import lax
from jax.experimental import pallas as pl
from jax.experimental.pallas import tpu as pltpu
from jax.sharding import PartitionSpec as P

LAYERS = 2
HALVES = 2
OFFSETS = 9
MESH = pl.DeviceIdType.MESH
BF = jnp.bfloat16
F32 = jnp.float32
ROWS = 16
LANES = 128
RANK = 32


def iota(shape, dim):
    return lax.broadcasted_iota(jnp.int32, shape, dim)


def one(condition, kind=F32):
    return jnp.where(condition, 1.0, 0.0).astype(kind)


def dot(a, b):
    return jnp.dot(a, b, preferred_element_type=F32)


def dot_t(a, b):
    return lax.dot_general(a, b, (((1,), (1,)), ((), ())), preferred_element_type=F32)


def gelu(v):
    return 0.5 * v * (1.0 + lax.erf(v * 0.7071067811865476))


def kernel(
    wide_x,
    wide_y,
    cells_x,
    cells_y,
    count_ref,
    mask_ref,
    feat_ref,
    tiles_hbm,
    proj_ref,
    exp_ref,
    src_ref,
    own_ref,
    cell_ref,
    pair_ref,
    mix_ref,
    res_ref,
    tiles,
    wt,
    xe,
    basis,
    out,
    inbox,
    flat,
    sums,
    exp4,
    lab_out,
    lab_in,
    sel,
    idx,
    idx_s,
    near,
    live,
    tile_sem,
    idx_sem,
    send_sem,
    recv_sem,
    halo_send,
    halo_recv,
    lab_sem,
    row_sem,
):
    a, b = lax.axis_index("gx"), lax.axis_index("gy")
    count = wide_x * wide_y
    me = a * wide_y + b
    cells = cells_x * cells_y
    half = 2 * ROWS

    def peer(da, db):
        return lax.rem(a + da + wide_x, wide_x), lax.rem(b + db + wide_y, wide_y)

    def signal(sem, where):
        pl.semaphore_signal(sem, inc=1, device_id=where, device_id_type=MESH)

    barrier = pltpu.get_barrier_semaphore()
    for step in range(1, wide_y):
        signal(barrier, peer(0, step))
    for step in range(1, wide_x):
        signal(barrier, peer(step, 0))
    for da in (-1, 1):
        for db in (-1, 1):
            signal(barrier, peer(da, db))

    parts = tile_sem.shape[0]
    size = cells * OFFSETS // parts

    def tile_copy(n):
        rows = pl.ds(n * size, size)
        return pltpu.make_async_copy(tiles_hbm.at[rows], tiles.at[rows], tile_sem.at[n])

    for n in range(parts):
        tile_copy(n).start()

    lane = iota((1, LANES), 1)
    slot_of = (lane // RANK) % 2
    first_slot = slot_of == 0
    first_ch = lane < 2 * RANK

    for c in range(cells):
        i, j = c // cells_y, c % cells_y
        alive = one(lane < count_ref[i, j])
        live[pl.ds(c, 1), :] = alive
        xe[0, i + 1, j + 1] = (feat_ref[c].astype(F32) * alive).astype(BF)

    owner = own_ref[0]
    named = one(iota((count, LANES), 0) == owner)
    before = dot(named.astype(BF), one(iota((LANES, LANES), 0) < iota((LANES, LANES), 1), BF))
    slot0 = jnp.where(before < 0.5, named, 0.0)
    slots = (slot0.astype(BF), (named - slot0).astype(BF))
    source = jnp.broadcast_to(src_ref[0], (8, LANES)).astype(F32).astype(BF)
    target = cell_ref[0]
    labels = jnp.zeros((count, LANES), F32)
    for k in range(2):
        idx[k] = dot_t(source, slots[k]).astype(jnp.int32)
        wanted = one(iota((LANES, LANES), 0) == target + k * cells, BF)
        labels = labels + dot_t(slots[k], wanted)
    lab_out[...] = labels
    to_scalars = pltpu.make_async_copy(idx, idx_s, idx_sem)
    to_scalars.start()

    for k in range(2):
        for j in range(RANK * RANK // LANES):
            flat[pl.ds(k * 8 + j, count, stride=ROWS), :] = dot(
                slots[k], pair_ref[:, j * LANES : (j + 1) * LANES]
            )
    fold_row, fold_col = iota((2 * LANES, LANES), 0), iota((2 * LANES, LANES), 1)
    fold = one(
        (fold_row % RANK == fold_col % RANK) & (fold_row // LANES == (fold_col // RANK) % 2), BF
    )
    quarter = [one(lane // RANK == q) for q in range(4)]
    block = 8

    def place(n, carry):
        lhs = []
        for d in range(block):
            v = flat[pl.ds((n * block + d) * ROWS, ROWS), :]
            lhs.append(
                jnp.concatenate(
                    [
                        jnp.concatenate([v[k * 8 : k * 8 + 8] * q for q in quarter], axis=0)
                        for k in range(2)
                    ],
                    axis=1,
                )
            )
        got = dot(jnp.concatenate(lhs, axis=0).astype(BF), fold)
        for d in range(block):
            r = got[d * RANK : (d + 1) * RANK]
            for q in range(4):
                wt[n * block + d, q * RANK : (q + 1) * RANK, :] = (r * quarter[q]).astype(BF)
        return carry

    lax.fori_loop(0, count // block, place, 0)

    spread_row, spread_col = iota((RANK, LANES), 0), iota((RANK, LANES), 1) % RANK
    spread = one(spread_row == 4 * (spread_col % 8) + spread_col // 8, BF)

    def project(layer, halves):
        lo, rows = halves[0] * half, len(halves) * half

        def body(c, carry):
            x = xe[layer, c // cells_y + 1, lax.rem(c, cells_y) + 1, lo : lo + rows, :]
            coef = dot_t(x, proj_ref[c]).astype(BF)
            wide = dot(coef, spread)
            for n, h in enumerate(halves):
                top = wide[n * half : n * half + ROWS]
                low = wide[n * half + ROWS : (n + 1) * half]
                basis[h, c] = jnp.where(first_ch, top, low).astype(BF)
            return carry

        lax.fori_loop(0, cells, body, 0, unroll=4)

    project(0, (0, 1))
    for c in range(cells):
        exp4[c] = jnp.concatenate([exp_ref[c]] * 4, axis=0)

    links = [
        (1, 0, (cells_x, pl.ds(1, cells_y)), (0, pl.ds(1, cells_y))),
        (-1, 0, (1, pl.ds(1, cells_y)), (cells_x + 1, pl.ds(1, cells_y))),
        (0, 1, (pl.ds(1, cells_x), cells_y), (pl.ds(1, cells_x), 0)),
        (0, -1, (pl.ds(1, cells_x), 1), (pl.ds(1, cells_x), cells_y + 1)),
        (1, 1, (cells_x, cells_y), (0, 0)),
        (1, -1, (cells_x, 1), (0, cells_y + 1)),
        (-1, 1, (1, cells_y), (cells_x + 1, 0)),
        (-1, -1, (1, 1), (cells_x + 1, cells_y + 1)),
    ]

    def halo(layer, part, rows, n):
        da, db, (si, sj), (ti, tj) = links[n]
        return pltpu.make_async_remote_copy(
            src_ref=xe.at[layer, si, sj, rows],
            dst_ref=xe.at[layer, ti, tj, rows],
            send_sem=halo_send.at[part, n],
            recv_sem=halo_recv.at[part, n],
            device_id=peer(da, db),
            device_id_type=MESH,
        )

    everything = pl.ds(0, 2 * half)
    halo_parts = [(0, everything), (1, pl.ds(0, half)), (1, pl.ds(half, half))]

    def halo_start(part):
        layer, rows = halo_parts[part]
        for n in range(len(links)):
            halo(layer, part, rows, n).start()

    def halo_wait(part):
        layer, rows = halo_parts[part]
        for n in range(len(links)):
            halo(layer, part, rows, n).wait_recv()

    pl.semaphore_wait(barrier, wide_x + wide_y - 2 + 4)
    for step in range(1, wide_x):
        signal(row_sem, peer(step, 0))
    halo_start(0)
    to_scalars.wait()

    def other_of(step):
        return lax.rem(me + 1 + step, count)

    def terms(rounds, halves):
        def body(n, carry):
            for d in range(block):
                o = other_of(n * block + d)
                s0, s1 = [lax.clamp(0, idx_s[k, 0, o], cells - 1) for k in range(2)]
                lhs = jnp.concatenate(
                    [jnp.where(first_slot, basis[h, s0], basis[h, s1]) for h in halves], axis=0
                )
                got = dot(lhs, wt[o]).astype(BF)
                for m, r in enumerate(rounds):
                    out[r, o] = got[m * ROWS : (m + 1) * ROWS]
            return carry

        lax.fori_loop(0, count // block, body, 0)

    def send(r):
        def body(step, carry):
            o = other_of(step)
            pltpu.make_async_remote_copy(
                src_ref=out.at[r, o],
                dst_ref=inbox.at[r, me],
                send_sem=send_sem.at[r],
                recv_sem=recv_sem.at[r],
                device_id=(o // wide_y, lax.rem(o, wide_y)),
                device_id_type=MESH,
            ).start()
            return carry

        lax.fori_loop(0, count - 1, body, 0)
        pltpu.make_async_copy(out.at[r, me], inbox.at[r, me], recv_sem.at[r]).start()

    def send_labels():
        def body(step, carry):
            o = other_of(step)
            pltpu.make_async_remote_copy(
                src_ref=lab_out.at[pl.ds(o, 1)],
                dst_ref=lab_in.at[pl.ds(me, 1)],
                send_sem=lab_sem.at[0],
                recv_sem=lab_sem.at[1],
                device_id=(o // wide_y, lax.rem(o, wide_y)),
                device_id_type=MESH,
            ).start()
            return carry

        lax.fori_loop(0, count - 1, body, 0)
        pltpu.make_async_copy(
            lab_out.at[pl.ds(me, 1)], lab_in.at[pl.ds(me, 1)], lab_sem.at[1]
        ).start()

    def receive(r):
        pltpu.make_async_copy(out.at[r], inbox.at[r], recv_sem.at[r]).wait()

    def near_field(layer):
        mix = mix_ref[layer]

        def body(c, carry):
            i, j = c // cells_y, lax.rem(c, cells_y)
            lhs = []
            for o in range(OFFSETS):
                active = mask_ref[i, j, o].astype(F32).astype(BF)
                lhs.append(xe[layer, i + o // 3, j + o % 3] * active)
            weights = tiles[pl.ds(c * OFFSETS, OFFSETS)].reshape(OFFSETS * LANES, LANES)
            near[c] = dot(jnp.concatenate(lhs, axis=1), weights) + dot(
                mix, xe[layer, i + 1, j + 1]
            )
            return carry

        lax.fori_loop(0, cells, body, 0)

    def gather(r):
        flat[: count * ROWS, :] = inbox[r].reshape(count * ROWS, LANES).astype(F32)
        chosen = sel[...]
        for row in range(ROWS):
            v = flat[pl.ds(row, count, stride=ROWS), :].astype(BF)
            got = dot(chosen, v)
            sums[pl.ds(row, cells, stride=ROWS), :] = got[:cells] + pltpu.roll(
                got[cells : 2 * cells], LANES - RANK, 1
            )

    def finish(layer, h):
        def body(c, carry):
            g = sums[pl.ds(c * ROWS, ROWS), :]
            lhs = jnp.concatenate(
                [jnp.where(first_slot & first_ch, g, 0.0), jnp.where(first_slot & ~first_ch, g, 0.0)],
                axis=0,
            ).astype(BF)
            hidden = near[c, h * half : (h + 1) * half, :] + dot(lhs, exp4[c])
            x = (gelu(hidden) * live[pl.ds(c, 1), :]).astype(BF)
            if layer + 1 < LAYERS:
                xe[layer + 1, c // cells_y + 1, lax.rem(c, cells_y) + 1, h * half : (h + 1) * half, :] = x
            else:
                res_ref[c, h * half : (h + 1) * half, :] = x
            return carry

        lax.fori_loop(0, cells, body, 0, unroll=2)

    terms((0, 1), (0, 1))
    pl.semaphore_wait(row_sem, wide_x - 1)
    send_labels()
    send(0)
    send(1)
    for n in range(parts):
        tile_copy(n).wait()
    halo_wait(0)
    near_field(0)
    pltpu.make_async_copy(lab_out, lab_in, lab_sem.at[1]).wait()
    sel[...] = jnp.transpose(lab_in[...])[: 2 * cells].astype(BF)
    for h in range(HALVES):
        receive(h)
        gather(h)
        finish(0, h)
        halo_start(1 + h)
        project(1, (h,))
        terms((2 + h,), (h,))
        send(2 + h)
    halo_wait(1)
    halo_wait(2)
    near_field(1)
    for h in range(HALVES):
        receive(2 + h)
        gather(2 + h)
        finish(1, h)

    rest = pl.ds(0, count - 1)
    for r in range(2 * LAYERS):
        pltpu.make_async_copy(out.at[r, rest], inbox.at[r, rest], send_sem.at[r]).wait()
    pltpu.make_async_copy(lab_out.at[rest], lab_in.at[rest], lab_sem.at[0]).wait()
    for part, (layer, rows) in enumerate(halo_parts):
        for n in range(len(links)):
            halo(layer, part, rows, n).wait_send()


def shards(
    features,
    cell_count,
    near_mask,
    near_tiles,
    projection_basis,
    expand_basis,
    far_source,
    far_owner,
    far_cell,
    distant_pair_matrix,
    mixing,
):
    cells_x, cells_y, chans, slots = features.shape
    rank = projection_basis.shape[2]
    cells = cells_x * cells_y
    pairs = far_source.shape[2]
    wide_x, wide_y = lax.axis_size("gx"), lax.axis_size("gy")
    count = wide_x * wide_y
    vmem = pl.BlockSpec(memory_space=pltpu.VMEM)
    smem = pl.BlockSpec(memory_space=pltpu.SMEM)
    hbm = pl.BlockSpec(memory_space=pl.ANY)
    rounds = 2 * LAYERS
    result = pl.pallas_call(
        functools.partial(kernel, wide_x, wide_y, cells_x, cells_y),
        out_shape=jax.ShapeDtypeStruct((cells, chans, slots), BF),
        in_specs=[smem, smem, vmem, hbm] + [vmem] * 7,
        out_specs=vmem,
        scratch_shapes=[
            pltpu.VMEM((cells * OFFSETS, slots, slots), BF),
            pltpu.VMEM((count, LANES, LANES), BF),
            pltpu.VMEM((LAYERS, cells_x + 2, cells_y + 2, chans, slots), BF),
            pltpu.VMEM((HALVES, cells, ROWS, LANES), BF),
            pltpu.VMEM((rounds, count, ROWS, LANES), BF),
            pltpu.VMEM((rounds, count, ROWS, LANES), BF),
            pltpu.VMEM((count * ROWS + ROWS, LANES), F32),
            pltpu.VMEM((cells * ROWS + ROWS, LANES), F32),
            pltpu.VMEM((cells, 4 * rank, slots), BF),
            pltpu.VMEM((count, LANES), F32),
            pltpu.VMEM((count, LANES), F32),
            pltpu.VMEM((2 * cells, count), BF),
            pltpu.VMEM((2, 8, LANES), jnp.int32),
            pltpu.SMEM((2, 8, LANES), jnp.int32),
            pltpu.VMEM((cells, chans, slots), F32),
            pltpu.VMEM((cells, slots), F32),
            pltpu.SemaphoreType.DMA((4,)),
            pltpu.SemaphoreType.DMA,
            pltpu.SemaphoreType.DMA((rounds,)),
            pltpu.SemaphoreType.DMA((rounds,)),
            pltpu.SemaphoreType.DMA((3, 8)),
            pltpu.SemaphoreType.DMA((3, 8)),
            pltpu.SemaphoreType.DMA((2,)),
            pltpu.SemaphoreType.REGULAR,
        ],
        compiler_params=pltpu.CompilerParams(
            collective_id=0, has_side_effects=True, vmem_limit_bytes=48 << 20
        ),
    )(
        cell_count,
        near_mask,
        features.reshape(cells, chans, slots),
        near_tiles.reshape(cells * OFFSETS, slots, slots),
        projection_basis.reshape(cells, rank, slots),
        expand_basis.reshape(cells, rank, slots),
        far_source.reshape(1, pairs),
        far_owner.reshape(1, pairs),
        far_cell.reshape(1, pairs),
        distant_pair_matrix.reshape(pairs, rank * rank),
        mixing,
    )
    return result.reshape(cells_x, cells_y, chans, slots)


def solution(mesh):
    placed = (
        P("gx", "gy", None, None),
        P("gx", "gy"),
        P("gx", "gy", None),
        P("gx", "gy", None, None, None),
        P("gx", "gy", None, None),
        P("gx", "gy", None, None),
        P("gx", "gy", None),
        P("gx", "gy", None, None),
        P("gx", "gy", None),
        P("gx", "gy", None, None),
        P(),
    )
    return jax.shard_map(
        shards, mesh=mesh, in_specs=placed, out_specs=P("gx", "gy", None, None), check_vma=False
    )
```

time: 127 us -> 83 us (0.65)
  the two profiles are of different devices: /device:TPU:7 before, /device:TPU:1 now
where the time goes in v2:
time: 83 us; the launch traced here: 82.6 us
  Pallas kernels  73.8 us (89%)
  local copies, waits for them, and re-layouts  8.8 us (11%)
    pallas_call x1, Pallas kernels, shards(): pl.pallas_call(functools.partial(kernel, wide_x, wide_y, cells_x, cells_y...  73.8 us
    unnamed x21, local copies, waits for them, and re-layouts  8.8 us

profile of v2, /device:TPU:1, one launch (start us, length us, event | category | flops | bytes accessed | tf_op | source)
XLA Modules:
  0.0 82.6 jit_solution(5457619583810010612)
XLA Ops:
  0.0 0.0 copy-start
  0.0 1.0 %copy-done = bf16[4,8,64,128]{3,2,1,0:T(8,128)(2,1)S(1)} copy-done((bf16[4,8,64,128]{3,2,1,0:T(8,128)(2,1)S(1)}, bf16[4,8,64,128]{3,2,1,0:T(8,128)(2,1)}, u32[]{:S(2)}) %copy-start) | copy-done | bytes 524312
  1.0 0.0 copy-start.1
  1.0 0.9 %copy-done.1 = bf16[4,8,32,128]{3,2,1,0:T(8,128)(2,1)S(1)} copy-done((bf16[4,8,32,128]{3,2,1,0:T(8,128)(2,1)S(1)}, bf16[4,8,32,128]{3,2,1,0:T(8,128)(2,1)}, u32[]{:S(2)}) %copy-start.1) | copy-done | bytes 262168
  2.0 0.0 copy-start.2
  2.0 0.9 %copy-done.2 = bf16[4,8,32,128]{3,2,1,0:T(8,128)(2,1)S(1)} copy-done((bf16[4,8,32,128]{3,2,1,0:T(8,128)(2,1)S(1)}, bf16[4,8,32,128]{3,2,1,0:T(8,128)(2,1)}, u32[]{:S(2)}) %copy-start.2) | copy-done | bytes 262168
  2.9 0.0 copy-start.3
  2.9 0.9 %copy-done.3 = bf16[1,1,128,1024]{3,2,1,0:T(8,128)(2,1)S(1)} copy-done((bf16[1,1,128,1024]{3,2,1,0:T(8,128)(2,1)S(1)}, bf16[1,1,128,1024]{3,2,1,0:T(8,128)(2,1)}, u32[]{:S(2)}) %copy-start.3) | copy-done | bytes 262168
  3.9 0.0 copy-start.4
  3.9 0.8 copy-done.4
  4.7 0.0 copy-start.5
  4.7 0.7 copy-done.5
  5.4 0.0 copy-start.6
  5.4 0.7 copy-done.6
  6.1 0.0 copy-start.7
  6.1 0.7 copy-done.7
  6.7 0.0 copy-start.8
  6.7 0.7 copy-done.8
  7.4 0.0 copy-start.9
  7.4 0.7 copy-done.9
  8.0 73.8 %shard_map.109 = bf16[32,64,128]{2,1,0:T(8,128)(2,1)S(1)} custom-call(s32[4,8]{1,0:T(4,128)S(1)} %copy-done.6, s32[4,8,9]{2,1,0:T(8,128)S(1)} %copy-done.5, bf16[32,64,128]{2,1,0:T(8,128)(2,1)S(1)} %bitcast.10, bf16[288,128,128]{2,1,0:T(8,128)(2,1)} %bitcast.17, bf16[32,32,128]{2,1,0:T(8,128)(2,1)S(1)} %bitcast.11, bf16[32,32,128]{2,1,0:T(8,128)(2,1)S(1)} %bitcast.12, ...), custom_call_target="tpu_custom_call" | custom-call | tf_op jit(solution)/shard_map/pallas_call | solution.py:396
  81.8 0.8 copy.13
Async XLA Ops:
  0.0 1.0 %copy-start = (bf16[4,8,64,128]{3,2,1,0:T(8,128)(2,1)S(1)}, bf16[4,8,64,128]{3,2,1,0:T(8,128)(2,1)}, u32[]{:S(2)}) copy-start(bf16[4,8,64,128]{3,2,1,0:T(8,128)(2,1)} %param.11) | copy-start | bytes 1572868
  1.0 0.9 %copy-start.1 = (bf16[4,8,32,128]{3,2,1,0:T(8,128)(2,1)S(1)}, bf16[4,8,32,128]{3,2,1,0:T(8,128)(2,1)}, u32[]{:S(2)}) copy-start(bf16[4,8,32,128]{3,2,1,0:T(8,128)(2,1)} %param.15) | copy-start | bytes 786436
  2.0 0.9 %copy-start.2 = (bf16[4,8,32,128]{3,2,1,0:T(8,128)(2,1)S(1)}, bf16[4,8,32,128]{3,2,1,0:T(8,128)(2,1)}, u32[]{:S(2)}) copy-start(bf16[4,8,32,128]{3,2,1,0:T(8,128)(2,1)} %param.16) | copy-start | bytes 786436
  2.9 0.9 %copy-start.3 = (bf16[1,1,128,1024]{3,2,1,0:T(8,128)(2,1)S(1)}, bf16[1,1,128,1024]{3,2,1,0:T(8,128)(2,1)}, u32[]{:S(2)}) copy-start(bf16[1,1,128,1024]{3,2,1,0:T(8,128)(2,1)} %param.20) | copy-start | bytes 786436
  3.9 0.8 copy-start.4
  4.7 0.7 copy-start.5
  5.4 0.7 copy-start.6
  6.1 0.7 copy-start.7
  6.7 0.7 copy-start.8
  7.4 0.7 copy-start.9

commit v3 on v2

--- a/solution.py
+++ b/solution.py
@@ -43,10 +43,21 @@
     wide_y,
     cells_x,
     cells_y,
+    count_hbm,
+    mask_hbm,
+    feat_hbm,
+    tiles_hbm,
+    proj_hbm,
+    exp_hbm,
+    src_hbm,
+    own_hbm,
+    cell_hbm,
+    pair_hbm,
+    mix_hbm,
+    res_ref,
     count_ref,
     mask_ref,
     feat_ref,
-    tiles_hbm,
     proj_ref,
     exp_ref,
     src_ref,
@@ -54,7 +65,8 @@
     cell_ref,
     pair_ref,
     mix_ref,
-    res_ref,
+    proj4,
+    load_sem,
     tiles,
     wt,
     xe,
@@ -65,6 +77,8 @@
     sums,
     exp4,
     lab_out,
+    lab_mid,
+    lab_turn,
     lab_in,
     sel,
     idx,
@@ -92,6 +106,26 @@
     def signal(sem, where):
         pl.semaphore_signal(sem, inc=1, device_id=where, device_id_type=MESH)
 
+    loads = [
+        pltpu.make_async_copy(hbm, ref, load_sem.at[n])
+        for n, (hbm, ref) in enumerate(
+            [
+                (count_hbm, count_ref),
+                (feat_hbm, feat_ref),
+                (src_hbm, src_ref),
+                (own_hbm, own_ref),
+                (cell_hbm, cell_ref),
+                (pair_hbm, pair_ref),
+                (proj_hbm, proj_ref),
+                (exp_hbm, exp_ref),
+                (mask_hbm, mask_ref),
+                (mix_hbm, mix_ref),
+            ]
+        )
+    ]
+    for load in loads:
+        load.start()
+
     barrier = pltpu.get_barrier_semaphore()
     for step in range(1, wide_y):
         signal(barrier, peer(0, step))
@@ -116,12 +150,21 @@
     first_slot = slot_of == 0
     first_ch = lane < 2 * RANK
 
-    for c in range(cells):
-        i, j = c // cells_y, c % cells_y
+    for load in loads[:2]:
+        load.wait()
+
+    def enter(c, carry):
+        i, j = c // cells_y, lax.rem(c, cells_y)
         alive = one(lane < count_ref[i, j])
         live[pl.ds(c, 1), :] = alive
         xe[0, i + 1, j + 1] = (feat_ref[c].astype(F32) * alive).astype(BF)
-
+        return carry
+
+    with jax.named_scope("enter"):
+        lax.fori_loop(0, cells, enter, 0, unroll=4)
+
+    for load in loads[2:]:
+        load.wait()
     owner = own_ref[0]
     named = one(iota((count, LANES), 0) == owner)
     before = dot(named.astype(BF), one(iota((LANES, LANES), 0) < iota((LANES, LANES), 1), BF))
@@ -134,7 +177,9 @@
         idx[k] = dot_t(source, slots[k]).astype(jnp.int32)
         wanted = one(iota((LANES, LANES), 0) == target + k * cells, BF)
         labels = labels + dot_t(slots[k], wanted)
-    lab_out[...] = labels
+    by_row, by_col = iota((count, LANES), 0), iota((count, LANES), 1)
+    by_column = one(by_col == by_row % wide_x * wide_y + by_row // wide_x, BF)
+    lab_out[...] = dot(by_column, labels.astype(BF))
     to_scalars = pltpu.make_async_copy(idx, idx_s, idx_sem)
     to_scalars.start()
 
@@ -148,6 +193,7 @@
         (fold_row % RANK == fold_col % RANK) & (fold_row // LANES == (fold_col // RANK) % 2), BF
     )
     quarter = [one(lane // RANK == q) for q in range(4)]
+    quarter_bf = [q.astype(BF) for q in quarter]
     block = 8
 
     def place(n, carry):
@@ -163,36 +209,15 @@
                     axis=1,
                 )
             )
-        got = dot(jnp.concatenate(lhs, axis=0).astype(BF), fold)
+        got = dot(jnp.concatenate(lhs, axis=0).astype(BF), fold).astype(BF)
         for d in range(block):
             r = got[d * RANK : (d + 1) * RANK]
             for q in range(4):
-                wt[n * block + d, q * RANK : (q + 1) * RANK, :] = (r * quarter[q]).astype(BF)
+                wt[n * block + d, q * RANK : (q + 1) * RANK, :] = r * quarter_bf[q]
         return carry
 
-    lax.fori_loop(0, count // block, place, 0)
-
-    spread_row, spread_col = iota((RANK, LANES), 0), iota((RANK, LANES), 1) % RANK
-    spread = one(spread_row == 4 * (spread_col % 8) + spread_col // 8, BF)
-
-    def project(layer, halves):
-        lo, rows = halves[0] * half, len(halves) * half
-
-        def body(c, carry):
-            x = xe[layer, c // cells_y + 1, lax.rem(c, cells_y) + 1, lo : lo + rows, :]
-            coef = dot_t(x, proj_ref[c]).astype(BF)
-            wide = dot(coef, spread)
-            for n, h in enumerate(halves):
-                top = wide[n * half : n * half + ROWS]
-                low = wide[n * half + ROWS : (n + 1) * half]
-                basis[h, c] = jnp.where(first_ch, top, low).astype(BF)
-            return carry
-
-        lax.fori_loop(0, cells, body, 0, unroll=4)
-
-    project(0, (0, 1))
-    for c in range(cells):
-        exp4[c] = jnp.concatenate([exp_ref[c]] * 4, axis=0)
+    with jax.named_scope("place"):
+        lax.fori_loop(0, count // block, place, 0, unroll=2)
 
     links = [
         (1, 0, (cells_x, pl.ds(1, cells_y)), (0, pl.ds(1, cells_y))),
@@ -229,19 +254,99 @@
         for n in range(len(links)):
             halo(layer, part, rows, n).wait_recv()
 
-    pl.semaphore_wait(barrier, wide_x + wide_y - 2 + 4)
+    def labels_along_y():
+        for step in range(1, wide_y):
+            there = peer(0, step)
+            pltpu.make_async_remote_copy(
+                src_ref=lab_out.at[pl.ds(pl.multiple_of(there[1] * wide_x, wide_x), wide_x)],
+                dst_ref=lab_mid.at[pl.ds(pl.multiple_of(b * wide_x, wide_x), wide_x)],
+                send_sem=lab_sem.at[0],
+                recv_sem=lab_sem.at[1],
+                device_id=there,
+                device_id_type=MESH,
+            ).start()
+        mine = pl.ds(pl.multiple_of(b * wide_x, wide_x), wide_x)
+        lab_mid[mine, :] = lab_out[mine, :]
+
+    def labels_along_x():
+        some = pl.ds(0, count - wide_x)
+        pltpu.make_async_copy(lab_out.at[some], lab_mid.at[some], lab_sem.at[1]).wait()
+        lab_turn[...] = lax.dot_general(
+            by_column,
+            lab_mid[...].astype(BF),
+            (((0,), (0,)), ((), ())),
+            preferred_element_type=F32,
+        )
+        for step in range(1, wide_x):
+            there = peer(step, 0)
+            pltpu.make_async_remote_copy(
+                src_ref=lab_turn.at[pl.ds(pl.multiple_of(there[0] * wide_y, wide_y), wide_y)],
+                dst_ref=lab_in.at[pl.ds(pl.multiple_of(a * wide_y, wide_y), wide_y)],
+                send_sem=lab_sem.at[2],
+                recv_sem=lab_sem.at[3],
+                device_id=there,
+                device_id_type=MESH,
+            ).start()
+        mine = pl.ds(pl.multiple_of(a * wide_y, wide_y), wide_y)
+        lab_in[mine, :] = lab_turn[mine, :]
+
+    with jax.named_scope("barrier_near"):
+        pl.semaphore_wait(barrier, wide_x + wide_y - 2 + 4)
     for step in range(1, wide_x):
         signal(row_sem, peer(step, 0))
     halo_start(0)
+    labels_along_y()
+
+    spread_row, spread_col = iota((LANES, RANK), 0) % RANK, iota((LANES, RANK), 1)
+    spread = one(spread_col == 4 * (spread_row % 8) + spread_row // 8, BF)
+
+    def widen(c, carry):
+        proj4[c] = dot(spread, proj_ref[c]).astype(BF)
+        exp4[c] = jnp.concatenate([exp_ref[c]] * 4, axis=0)
+        return carry
+
+    with jax.named_scope("widen"):
+        lax.fori_loop(0, cells, widen, 0, unroll=4)
+
+    def project(layer, halves):
+        lo, rows = halves[0] * half, len(halves) * half
+
+        def body(c, carry):
+            x = xe[layer, c // cells_y + 1, lax.rem(c, cells_y) + 1, lo : lo + rows, :]
+            wide = dot_t(x, proj4[c])
+            for n, h in enumerate(halves):
+                top = wide[n * half : n * half + ROWS]
+                low = wide[n * half + ROWS : (n + 1) * half]
+                basis[h, c] = jnp.where(first_ch, top, low).astype(BF)
+            return carry
+
+        lax.fori_loop(0, cells, body, 0, unroll=8)
+
+    with jax.named_scope("project"):
+        project(0, (0, 1))
+
     to_scalars.wait()
 
-    def other_of(step):
-        return lax.rem(me + 1 + step, count)
+    def send_one(r, step):
+        o = lax.rem(me + step, count)
+        pltpu.make_async_remote_copy(
+            src_ref=out.at[r, o],
+            dst_ref=inbox.at[r, me],
+            send_sem=send_sem.at[r],
+            recv_sem=recv_sem.at[r],
+            device_id=(o // wide_y, lax.rem(o, wide_y)),
+            device_id_type=MESH,
+        ).start()
+
+    def send_own(r):
+        pltpu.make_async_copy(out.at[r, me], inbox.at[r, me], recv_sem.at[r]).start()
+
+    group = 16
 
     def terms(rounds, halves):
         def body(n, carry):
-            for d in range(block):
-                o = other_of(n * block + d)
+            for d in range(group):
+                o = lax.rem(me + n * group + d, count)
                 s0, s1 = [lax.clamp(0, idx_s[k, 0, o], cells - 1) for k in range(2)]
                 lhs = jnp.concatenate(
                     [jnp.where(first_slot, basis[h, s0], basis[h, s1]) for h in halves], axis=0
@@ -249,43 +354,28 @@
                 got = dot(lhs, wt[o]).astype(BF)
                 for m, r in enumerate(rounds):
                     out[r, o] = got[m * ROWS : (m + 1) * ROWS]
+
+            @pl.when(n == 0)
+            def _():
+                for r in rounds:
+                    send_own(r)
+
+            @pl.when(n > 0)
+            def _():
+                send_one(rounds[0], n * group)
+
+            for d in range(1, group):
+                send_one(rounds[0], n * group + d)
             return carry
 
-        lax.fori_loop(0, count // block, body, 0)
+        lax.fori_loop(0, count // group, body, 0)
 
     def send(r):
         def body(step, carry):
-            o = other_of(step)
-            pltpu.make_async_remote_copy(
-                src_ref=out.at[r, o],
-                dst_ref=inbox.at[r, me],
-                send_sem=send_sem.at[r],
-                recv_sem=recv_sem.at[r],
-                device_id=(o // wide_y, lax.rem(o, wide_y)),
-                device_id_type=MESH,
-            ).start()
+            send_one(r, step)
             return carry
 
-        lax.fori_loop(0, count - 1, body, 0)
-        pltpu.make_async_copy(out.at[r, me], inbox.at[r, me], recv_sem.at[r]).start()
-
-    def send_labels():
-        def body(step, carry):
-            o = other_of(step)
-            pltpu.make_async_remote_copy(
-                src_ref=lab_out.at[pl.ds(o, 1)],
-                dst_ref=lab_in.at[pl.ds(me, 1)],
-                send_sem=lab_sem.at[0],
-                recv_sem=lab_sem.at[1],
-                device_id=(o // wide_y, lax.rem(o, wide_y)),
-                device_id_type=MESH,
-            ).start()
-            return carry
-
-        lax.fori_loop(0, count - 1, body, 0)
-        pltpu.make_async_copy(
-            lab_out.at[pl.ds(me, 1)], lab_in.at[pl.ds(me, 1)], lab_sem.at[1]
-        ).start()
+        lax.fori_loop(1, count, body, 0)
 
     def receive(r):
         pltpu.make_async_copy(out.at[r], inbox.at[r], recv_sem.at[r]).wait()
@@ -305,7 +395,7 @@
             )
             return carry
 
-        lax.fori_loop(0, cells, body, 0)
+        lax.fori_loop(0, cells, body, 0, unroll=2)
 
     def gather(r):
         flat[: count * ROWS, :] = inbox[r].reshape(count * ROWS, LANES).astype(F32)
@@ -332,39 +422,61 @@
                 res_ref[c, h * half : (h + 1) * half, :] = x
             return carry
 
-        lax.fori_loop(0, cells, body, 0, unroll=2)
-
-    terms((0, 1), (0, 1))
-    pl.semaphore_wait(row_sem, wide_x - 1)
-    send_labels()
-    send(0)
-    send(1)
-    for n in range(parts):
-        tile_copy(n).wait()
-    halo_wait(0)
-    near_field(0)
-    pltpu.make_async_copy(lab_out, lab_in, lab_sem.at[1]).wait()
-    sel[...] = jnp.transpose(lab_in[...])[: 2 * cells].astype(BF)
+        lax.fori_loop(0, cells, body, 0, unroll=4)
+
+    scope = jax.named_scope
+    with scope("barrier_all"):
+        pl.semaphore_wait(row_sem, wide_x - 1)
+    with scope("terms"):
+        terms((0, 1), (0, 1))
+    with scope("labels"):
+        labels_along_x()
+    with scope("send_terms"):
+        send(1)
+    with scope("wait_tiles"):
+        for n in range(parts):
+            tile_copy(n).wait()
+    with scope("wait_halo"):
+        halo_wait(0)
+    with scope("near"):
+        near_field(0)
+    with scope("wait_labels"):
+        some = pl.ds(0, count - wide_y)
+        pltpu.make_async_copy(lab_turn.at[some], lab_in.at[some], lab_sem.at[3]).wait()
+        sel[...] = jnp.transpose(lab_in[...])[: 2 * cells].astype(BF)
     for h in range(HALVES):
-        receive(h)
-        gather(h)
-        finish(0, h)
-        halo_start(1 + h)
-        project(1, (h,))
-        terms((2 + h,), (h,))
-        send(2 + h)
-    halo_wait(1)
-    halo_wait(2)
-    near_field(1)
+        with scope("wait_terms"):
+            receive(h)
+        with scope("gather"):
+            gather(h)
+        with scope("finish"):
+            finish(0, h)
+        with scope("halo"):
+            halo_start(1 + h)
+        with scope("project"):
+            project(1, (h,))
+        with scope("terms"):
+            terms((2 + h,), (h,))
+    with scope("wait_halo"):
+        halo_wait(1)
+        halo_wait(2)
+    with scope("near"):
+        near_field(1)
     for h in range(HALVES):
-        receive(2 + h)
-        gather(2 + h)
-        finish(1, h)
+        with scope("wait_terms"):
+            receive(2 + h)
+        with scope("gather"):
+            gather(2 + h)
+        with scope("finish"):
+            finish(1, h)
 
     rest = pl.ds(0, count - 1)
     for r in range(2 * LAYERS):
         pltpu.make_async_copy(out.at[r, rest], inbox.at[r, rest], send_sem.at[r]).wait()
-    pltpu.make_async_copy(lab_out.at[rest], lab_in.at[rest], lab_sem.at[0]).wait()
+    some = pl.ds(0, count - wide_x)
+    pltpu.make_async_copy(lab_out.at[some], lab_mid.at[some], lab_sem.at[0]).wait()
+    some = pl.ds(0, count - wide_y)
+    pltpu.make_async_copy(lab_turn.at[some], lab_in.at[some], lab_sem.at[2]).wait()
     for part, (layer, rows) in enumerate(halo_parts):
         for n in range(len(links)):
             halo(layer, part, rows, n).wait_send()
@@ -390,15 +502,26 @@
     wide_x, wide_y = lax.axis_size("gx"), lax.axis_size("gy")
     count = wide_x * wide_y
     vmem = pl.BlockSpec(memory_space=pltpu.VMEM)
-    smem = pl.BlockSpec(memory_space=pltpu.SMEM)
-    hbm = pl.BlockSpec(memory_space=pl.ANY)
+    hbm = pl.BlockSpec(memory_space=pltpu.HBM)
     rounds = 2 * LAYERS
     result = pl.pallas_call(
         functools.partial(kernel, wide_x, wide_y, cells_x, cells_y),
         out_shape=jax.ShapeDtypeStruct((cells, chans, slots), BF),
-        in_specs=[smem, smem, vmem, hbm] + [vmem] * 7,
+        in_specs=[hbm] * 11,
         out_specs=vmem,
         scratch_shapes=[
+            pltpu.SMEM((cells_x, cells_y), jnp.int32),
+            pltpu.SMEM((cells_x, cells_y, OFFSETS), jnp.int32),
+            pltpu.VMEM((cells, chans, slots), BF),
+            pltpu.VMEM((cells, rank, slots), BF),
+            pltpu.VMEM((cells, rank, slots), BF),
+            pltpu.VMEM((1, pairs), jnp.int32),
+            pltpu.VMEM((1, pairs), jnp.int32),
+            pltpu.VMEM((1, pairs), jnp.int32),
+            pltpu.VMEM((pairs, rank * rank), BF),
+            pltpu.VMEM((LAYERS, chans, chans), BF),
+            pltpu.VMEM((cells, 4 * rank, slots), BF),
+            pltpu.SemaphoreType.DMA((10,)),
             pltpu.VMEM((cells * OFFSETS, slots, slots), BF),
             pltpu.VMEM((count, LANES, LANES), BF),
             pltpu.VMEM((LAYERS, cells_x + 2, cells_y + 2, chans, slots), BF),
@@ -408,6 +531,8 @@
             pltpu.VMEM((count * ROWS + ROWS, LANES), F32),
             pltpu.VMEM((cells * ROWS + ROWS, LANES), F32),
             pltpu.VMEM((cells, 4 * rank, slots), BF),
+            pltpu.VMEM((count, LANES), F32),
+            pltpu.VMEM((count, LANES), F32),
             pltpu.VMEM((count, LANES), F32),
             pltpu.VMEM((count, LANES), F32),
             pltpu.VMEM((2 * cells, count), BF),
@@ -421,11 +546,11 @@
             pltpu.SemaphoreType.DMA((rounds,)),
             pltpu.SemaphoreType.DMA((3, 8)),
             pltpu.SemaphoreType.DMA((3, 8)),
-            pltpu.SemaphoreType.DMA((2,)),
+            pltpu.SemaphoreType.DMA((4,)),
             pltpu.SemaphoreType.REGULAR,
         ],
         compiler_params=pltpu.CompilerParams(
-            collective_id=0, has_side_effects=True, vmem_limit_bytes=48 << 20
+            collective_id=0, has_side_effects=True, vmem_limit_bytes=56 << 20
         ),
     )(
         cell_count,

time: 83 us -> 52.9 us (0.64)
  the two profiles are of different devices: /device:TPU:1 before, /device:TPU:30 now
where the time goes in v3:
time: 52.9 us; the launch traced here: 52.8 us
  Pallas kernels  50.9 us (96%)
  local copies, waits for them, and re-layouts  1.87 us (4%)
    pallas_call x1, Pallas kernels, shards(): pl.pallas_call(functools.partial(kernel, wide_x, wide_y, cells_x, cells_y...  50.9 us
    unnamed x1, local copies, waits for them, and re-layouts  1.87 us

profile of v3, /device:TPU:30, one launch (start us, length us, event | category | flops | bytes accessed | tf_op | source)
XLA Modules:
  0.0 52.8 jit_solution(14817994174185311832)
XLA Ops:
  0.0 50.9 %shard_map.109 = bf16[32,64,128]{2,1,0:T(8,128)(2,1)} custom-call(s32[4,8]{1,0:T(4,128)} %count_hbm.1, s32[4,8,9]{2,1,0:T(8,128)} %mask_hbm.1, bf16[32,64,128]{2,1,0:T(8,128)(2,1)} %bitcast.11, bf16[288,128,128]{2,1,0:T(8,128)(2,1)} %bitcast.9, bf16[32,32,128]{2,1,0:T(8,128)(2,1)} %bitcast.12, bf16[32,32,128]{2,1,0:T(8,128)(2,1)} %bitcast.13, ...), custom_call_target="tpu_custom_call" | custom-call | tf_op jit(solution)/shard_map/pallas_call | solution.py:507
  50.9 1.9 %copy.13 = bf16[4,8,64,128]{3,2,1,0:T(8,128)(2,1)} copy(bf16[4,8,64,128]{3,2,1,0:T(8,128)(2,1)} %bitcast.10) | data formatting | bytes 1048576

commit v4 on v3

--- a/solution.py
+++ b/solution.py
@@ -54,7 +54,9 @@
     cell_hbm,
     pair_hbm,
     mix_hbm,
+    res_hbm,
     res_ref,
+    res_sem,
     count_ref,
     mask_ref,
     feat_ref,
@@ -131,9 +133,6 @@
         signal(barrier, peer(0, step))
     for step in range(1, wide_x):
         signal(barrier, peer(step, 0))
-    for da in (-1, 1):
-        for db in (-1, 1):
-            signal(barrier, peer(da, db))
 
     parts = tile_sem.shape[0]
     size = cells * OFFSETS // parts
@@ -217,7 +216,7 @@
         return carry
 
     with jax.named_scope("place"):
-        lax.fori_loop(0, count // block, place, 0, unroll=2)
+        lax.fori_loop(0, count // block, place, 0, unroll=4)
 
     links = [
         (1, 0, (cells_x, pl.ds(1, cells_y)), (0, pl.ds(1, cells_y))),
@@ -244,9 +243,9 @@
     everything = pl.ds(0, 2 * half)
     halo_parts = [(0, everything), (1, pl.ds(0, half)), (1, pl.ds(half, half))]
 
-    def halo_start(part):
+    def halo_start(part, some=range(8)):
         layer, rows = halo_parts[part]
-        for n in range(len(links)):
+        for n in some:
             halo(layer, part, rows, n).start()
 
     def halo_wait(part):
@@ -291,10 +290,10 @@
         lab_in[mine, :] = lab_turn[mine, :]
 
     with jax.named_scope("barrier_near"):
-        pl.semaphore_wait(barrier, wide_x + wide_y - 2 + 4)
+        pl.semaphore_wait(barrier, wide_x + wide_y - 2)
     for step in range(1, wide_x):
         signal(row_sem, peer(step, 0))
-    halo_start(0)
+    halo_start(0, range(4))
     labels_along_y()
 
     spread_row, spread_col = iota((LANES, RANK), 0) % RANK, iota((LANES, RANK), 1)
@@ -334,14 +333,14 @@
             dst_ref=inbox.at[r, me],
             send_sem=send_sem.at[r],
             recv_sem=recv_sem.at[r],
-            device_id=(o // wide_y, lax.rem(o, wide_y)),
-            device_id_type=MESH,
+            device_id=o,
+            device_id_type=pl.DeviceIdType.LOGICAL,
         ).start()
 
     def send_own(r):
         pltpu.make_async_copy(out.at[r, me], inbox.at[r, me], recv_sem.at[r]).start()
 
-    group = 16
+    group = 8
 
     def terms(rounds, halves):
         def body(n, carry):
@@ -371,20 +370,24 @@
         lax.fori_loop(0, count // group, body, 0)
 
     def send(r):
-        def body(step, carry):
-            send_one(r, step)
+        def body(n, carry):
+            for d in range(group):
+                send_one(r, n * group + d)
             return carry
 
-        lax.fori_loop(1, count, body, 0)
+        for d in range(1, group):
+            send_one(r, d)
+        lax.fori_loop(1, count // group, body, 0)
 
     def receive(r):
         pltpu.make_async_copy(out.at[r], inbox.at[r], recv_sem.at[r]).wait()
 
-    def near_field(layer):
+    def near_cells(layer, total, place_of):
         mix = mix_ref[layer]
 
-        def body(c, carry):
-            i, j = c // cells_y, lax.rem(c, cells_y)
+        def body(n, carry):
+            i, j = place_of(n)
+            c = i * cells_y + j
             lhs = []
             for o in range(OFFSETS):
                 active = mask_ref[i, j, o].astype(F32).astype(BF)
@@ -395,7 +398,21 @@
             )
             return carry
 
-        lax.fori_loop(0, cells, body, 0, unroll=2)
+        lax.fori_loop(0, total, body, 0, unroll=4)
+
+    def near_inner(layer):
+        wide = cells_y - 2
+        near_cells(
+            layer, (cells_x - 2) * wide, lambda n: (1 + lax.div(n, wide), 1 + lax.rem(n, wide))
+        )
+
+    def near_edge(layer):
+        near_cells(
+            layer, 2 * cells_y, lambda n: (lax.div(n, cells_y) * (cells_x - 1), lax.rem(n, cells_y))
+        )
+        near_cells(
+            layer, 2 * (cells_x - 2), lambda n: (1 + lax.div(n, 2), lax.rem(n, 2) * (cells_y - 1))
+        )
 
     def gather(r):
         flat[: count * ROWS, :] = inbox[r].reshape(count * ROWS, LANES).astype(F32)
@@ -407,26 +424,40 @@
                 got[cells : 2 * cells], LANES - RANK, 1
             )
 
+    def leave(h, n):
+        where = (pl.ds(n * block, block), pl.ds(h * half, half))
+        return pltpu.make_async_copy(res_ref.at[where], res_hbm.at[where], res_sem.at[h, n])
+
     def finish(layer, h):
-        def body(c, carry):
-            g = sums[pl.ds(c * ROWS, ROWS), :]
-            lhs = jnp.concatenate(
-                [jnp.where(first_slot & first_ch, g, 0.0), jnp.where(first_slot & ~first_ch, g, 0.0)],
-                axis=0,
-            ).astype(BF)
-            hidden = near[c, h * half : (h + 1) * half, :] + dot(lhs, exp4[c])
-            x = (gelu(hidden) * live[pl.ds(c, 1), :]).astype(BF)
-            if layer + 1 < LAYERS:
-                xe[layer + 1, c // cells_y + 1, lax.rem(c, cells_y) + 1, h * half : (h + 1) * half, :] = x
-            else:
-                res_ref[c, h * half : (h + 1) * half, :] = x
+        rows = slice(h * half, (h + 1) * half)
+
+        def body(n, carry):
+            for d in range(block):
+                c = n * block + d
+                g = sums[pl.ds(c * ROWS, ROWS), :]
+                lhs = jnp.concatenate(
+                    [
+                        jnp.where(first_slot & first_ch, g, 0.0),
+                        jnp.where(first_slot & ~first_ch, g, 0.0),
+                    ],
+                    axis=0,
+                ).astype(BF)
+                hidden = near[c, rows, :] + dot(lhs, exp4[c])
+                x = (gelu(hidden) * live[pl.ds(c, 1), :]).astype(BF)
+                if layer + 1 < LAYERS:
+                    xe[layer + 1, c // cells_y + 1, lax.rem(c, cells_y) + 1, rows, :] = x
+                else:
+                    res_ref[c, rows, :] = x
+            if layer + 1 == LAYERS:
+                leave(h, n).start()
             return carry
 
-        lax.fori_loop(0, cells, body, 0, unroll=4)
+        lax.fori_loop(0, cells // block, body, 0)
 
     scope = jax.named_scope
     with scope("barrier_all"):
         pl.semaphore_wait(row_sem, wide_x - 1)
+        halo_start(0, range(4, 8))
     with scope("terms"):
         terms((0, 1), (0, 1))
     with scope("labels"):
@@ -436,10 +467,12 @@
     with scope("wait_tiles"):
         for n in range(parts):
             tile_copy(n).wait()
+    with scope("near"):
+        near_inner(0)
     with scope("wait_halo"):
         halo_wait(0)
     with scope("near"):
-        near_field(0)
+        near_edge(0)
     with scope("wait_labels"):
         some = pl.ds(0, count - wide_y)
         pltpu.make_async_copy(lab_turn.at[some], lab_in.at[some], lab_sem.at[3]).wait()
@@ -457,19 +490,25 @@
             project(1, (h,))
         with scope("terms"):
             terms((2 + h,), (h,))
-    with scope("wait_halo"):
-        halo_wait(1)
-        halo_wait(2)
     with scope("near"):
-        near_field(1)
+        near_inner(1)
     for h in range(HALVES):
         with scope("wait_terms"):
             receive(2 + h)
         with scope("gather"):
             gather(2 + h)
+        if h == 0:
+            with scope("wait_halo"):
+                halo_wait(1)
+                halo_wait(2)
+            with scope("near"):
+                near_edge(1)
         with scope("finish"):
             finish(1, h)
 
+    for h in range(HALVES):
+        for n in range(cells // block):
+            leave(h, n).wait()
     rest = pl.ds(0, count - 1)
     for r in range(2 * LAYERS):
         pltpu.make_async_copy(out.at[r, rest], inbox.at[r, rest], send_sem.at[r]).wait()
@@ -501,15 +540,16 @@
     pairs = far_source.shape[2]
     wide_x, wide_y = lax.axis_size("gx"), lax.axis_size("gy")
     count = wide_x * wide_y
-    vmem = pl.BlockSpec(memory_space=pltpu.VMEM)
     hbm = pl.BlockSpec(memory_space=pltpu.HBM)
     rounds = 2 * LAYERS
     result = pl.pallas_call(
         functools.partial(kernel, wide_x, wide_y, cells_x, cells_y),
         out_shape=jax.ShapeDtypeStruct((cells, chans, slots), BF),
         in_specs=[hbm] * 11,
-        out_specs=vmem,
+        out_specs=hbm,
         scratch_shapes=[
+            pltpu.VMEM((cells, chans, slots), BF),
+            pltpu.SemaphoreType.DMA((HALVES, cells // 8)),
             pltpu.SMEM((cells_x, cells_y), jnp.int32),
             pltpu.SMEM((cells_x, cells_y, OFFSETS), jnp.int32),
             pltpu.VMEM((cells, chans, slots), BF),

time: 52.9 us -> 50.3 us (0.951)
  the two profiles are of different devices: /device:TPU:30 before, /device:TPU:1 now
where the time goes in v4:
time: 50.3 us; the launch traced here: 50.1 us
  Pallas kernels  48.2 us (96%)
  local copies, waits for them, and re-layouts  1.87 us (4%)
    pallas_call x1, Pallas kernels, shards(): pl.pallas_call(functools.partial(kernel, wide_x, wide_y, cells_x, cells_y...  48.2 us
    unnamed x1, local copies, waits for them, and re-layouts  1.87 us

profile of v4, /device:TPU:1, one launch (start us, length us, event | category | flops | bytes accessed | tf_op | source)
XLA Modules:
  0.0 50.1 jit_solution(15327109912967619207)
XLA Ops:
  0.0 48.2 %shard_map.109 = bf16[32,64,128]{2,1,0:T(8,128)(2,1)} custom-call(s32[4,8]{1,0:T(4,128)} %count_hbm.1, s32[4,8,9]{2,1,0:T(8,128)} %mask_hbm.1, bf16[32,64,128]{2,1,0:T(8,128)(2,1)} %bitcast.11, bf16[288,128,128]{2,1,0:T(8,128)(2,1)} %bitcast.9, bf16[32,32,128]{2,1,0:T(8,128)(2,1)} %bitcast.12, bf16[32,32,128]{2,1,0:T(8,128)(2,1)} %bitcast.13, ...), custom_call_target="tpu_custom_call" | custom-call | tf_op jit(solution)/shard_map/pallas_call | solution.py:545
  48.2 1.9 %copy.13 = bf16[4,8,64,128]{3,2,1,0:T(8,128)(2,1)} copy(bf16[4,8,64,128]{3,2,1,0:T(8,128)(2,1)} %bitcast.10) | data formatting | bytes 1048576

commit v5 on v4

--- a/solution.py
+++ b/solution.py
@@ -10,7 +10,7 @@
 LAYERS = 2
 HALVES = 2
 OFFSETS = 9
-MESH = pl.DeviceIdType.MESH
+FLAT = pl.DeviceIdType.LOGICAL
 BF = jnp.bfloat16
 F32 = jnp.float32
 ROWS = 16
@@ -105,8 +105,11 @@
     def peer(da, db):
         return lax.rem(a + da + wide_x, wide_x), lax.rem(b + db + wide_y, wide_y)
 
+    def flat_id(where):
+        return where[0] * wide_y + where[1]
+
     def signal(sem, where):
-        pl.semaphore_signal(sem, inc=1, device_id=where, device_id_type=MESH)
+        pl.semaphore_signal(sem, inc=1, device_id=flat_id(where), device_id_type=FLAT)
 
     loads = [
         pltpu.make_async_copy(hbm, ref, load_sem.at[n])
@@ -236,8 +239,8 @@
             dst_ref=xe.at[layer, ti, tj, rows],
             send_sem=halo_send.at[part, n],
             recv_sem=halo_recv.at[part, n],
-            device_id=peer(da, db),
-            device_id_type=MESH,
+            device_id=flat_id(peer(da, db)),
+            device_id_type=FLAT,
         )
 
     everything = pl.ds(0, 2 * half)
@@ -261,8 +264,8 @@
                 dst_ref=lab_mid.at[pl.ds(pl.multiple_of(b * wide_x, wide_x), wide_x)],
                 send_sem=lab_sem.at[0],
                 recv_sem=lab_sem.at[1],
-                device_id=there,
-                device_id_type=MESH,
+                device_id=flat_id(there),
+                device_id_type=FLAT,
             ).start()
         mine = pl.ds(pl.multiple_of(b * wide_x, wide_x), wide_x)
         lab_mid[mine, :] = lab_out[mine, :]
@@ -283,8 +286,8 @@
                 dst_ref=lab_in.at[pl.ds(pl.multiple_of(a * wide_y, wide_y), wide_y)],
                 send_sem=lab_sem.at[2],
                 recv_sem=lab_sem.at[3],
-                device_id=there,
-                device_id_type=MESH,
+                device_id=flat_id(there),
+                device_id_type=FLAT,
             ).start()
         mine = pl.ds(pl.multiple_of(a * wide_y, wide_y), wide_y)
         lab_in[mine, :] = lab_turn[mine, :]
@@ -334,7 +337,7 @@
             send_sem=send_sem.at[r],
             recv_sem=recv_sem.at[r],
             device_id=o,
-            device_id_type=pl.DeviceIdType.LOGICAL,
+            device_id_type=FLAT,
         ).start()
 
     def send_own(r):
@@ -367,7 +370,7 @@
                 send_one(rounds[0], n * group + d)
             return carry
 
-        lax.fori_loop(0, count // group, body, 0)
+        lax.fori_loop(0, count // group, body, 0, unroll=2)
 
     def send(r):
         def body(n, carry):
@@ -452,7 +455,7 @@
                 leave(h, n).start()
             return carry
 
-        lax.fori_loop(0, cells // block, body, 0)
+        lax.fori_loop(0, cells // block, body, 0, unroll=2)
 
     scope = jax.named_scope
     with scope("barrier_all"):

time: 50.3 us -> 49.7 us (0.988)
  Pallas kernels: 48.2 us -> 47.6 us
    pallas_call x1, Pallas kernels: 48.2 us -> 47.6 us  [shards(): pl.pallas_call(functools.partial(kernel, wide_x, wide_y, cells_x, cells_y...]
where the time goes in v5:
time: 49.7 us; the launch traced here: 49.5 us
  Pallas kernels  47.6 us (96%)
  local copies, waits for them, and re-layouts  1.87 us (4%)
    pallas_call x1, Pallas kernels, shards(): pl.pallas_call(functools.partial(kernel, wide_x, wide_y, cells_x, cells_y...  47.6 us
    unnamed x1, local copies, waits for them, and re-layouts  1.87 us

profile of v5, /device:TPU:1, one launch (start us, length us, event | category | flops | bytes accessed | tf_op | source)
XLA Modules:
  0.0 49.5 jit_solution(7385546725275769329)
XLA Ops:
  0.0 47.6 %shard_map.109 = bf16[32,64,128]{2,1,0:T(8,128)(2,1)} custom-call(s32[4,8]{1,0:T(4,128)} %count_hbm.1, s32[4,8,9]{2,1,0:T(8,128)} %mask_hbm.1, bf16[32,64,128]{2,1,0:T(8,128)(2,1)} %bitcast.11, bf16[288,128,128]{2,1,0:T(8,128)(2,1)} %bitcast.9, bf16[32,32,128]{2,1,0:T(8,128)(2,1)} %bitcast.12, bf16[32,32,128]{2,1,0:T(8,128)(2,1)} %bitcast.13, ...), custom_call_target="tpu_custom_call" | custom-call | tf_op jit(solution)/shard_map/pallas_call | solution.py:548
  47.6 1.9 %copy.13 = bf16[4,8,64,128]{3,2,1,0:T(8,128)(2,1)} copy(bf16[4,8,64,128]{3,2,1,0:T(8,128)(2,1)} %bitcast.10) | data formatting | bytes 1048576

commit v6 on v5

--- a/solution.py
+++ b/solution.py
@@ -322,7 +322,7 @@
                 basis[h, c] = jnp.where(first_ch, top, low).astype(BF)
             return carry
 
-        lax.fori_loop(0, cells, body, 0, unroll=8)
+        lax.fori_loop(0, cells, body, 0, unroll=16)
 
     with jax.named_scope("project"):
         project(0, (0, 1))
@@ -455,7 +455,7 @@
                 leave(h, n).start()
             return carry
 
-        lax.fori_loop(0, cells // block, body, 0, unroll=2)
+        lax.fori_loop(0, cells // block, body, 0, unroll=4)
 
     scope = jax.named_scope
     with scope("barrier_all"):

time: 49.7 us -> 49.3 us (level)
  no operation moved by 1% of the time
where the time goes in v6:
time: 49.3 us; the launch traced here: 49.1 us
  Pallas kernels  47.3 us (96%)
  local copies, waits for them, and re-layouts  1.87 us (4%)
    pallas_call x1, Pallas kernels, shards(): pl.pallas_call(functools.partial(kernel, wide_x, wide_y, cells_x, cells_y...  47.3 us
    unnamed x1, local copies, waits for them, and re-layouts  1.87 us

profile of v6, /device:TPU:1, one launch (start us, length us, event | category | flops | bytes accessed | tf_op | source)
XLA Modules:
  0.0 49.1 jit_solution(18444879691021700261)
XLA Ops:
  0.0 47.3 %shard_map.109 = bf16[32,64,128]{2,1,0:T(8,128)(2,1)} custom-call(s32[4,8]{1,0:T(4,128)} %count_hbm.1, s32[4,8,9]{2,1,0:T(8,128)} %mask_hbm.1, bf16[32,64,128]{2,1,0:T(8,128)(2,1)} %bitcast.11, bf16[288,128,128]{2,1,0:T(8,128)(2,1)} %bitcast.9, bf16[32,32,128]{2,1,0:T(8,128)(2,1)} %bitcast.12, bf16[32,32,128]{2,1,0:T(8,128)(2,1)} %bitcast.13, ...), custom_call_target="tpu_custom_call" | custom-call | tf_op jit(solution)/shard_map/pallas_call | solution.py:548
  47.3 1.9 %copy.13 = bf16[4,8,64,128]{3,2,1,0:T(8,128)(2,1)} copy(bf16[4,8,64,128]{3,2,1,0:T(8,128)(2,1)} %bitcast.10) | data formatting | bytes 1048576
